TPU v7x, 512 devices: a whole 4x8x8 slice. The times are simulated.
512 devices in a mesh: rp: 32 (over z, x_hi, core), re: 16 (over y, x_lo).
Axes of the slice: x: 4 (x_hi: 2, x_lo: 2; x = x_hi * 2 + x_lo), y: 8, z: 8, core: 2. Of those that a mesh axis runs over, the one named last changes fastest.
Arguments:
- wannier_coupling: bfloat16 [64, 128, 6400], P('re', 'rp'), may hold values from -0.0029296875 to 0.0029296875
- phonon_lattice: int32 [128, 3], P('rp'), may hold values from -6 to 6
- phonon_degeneracy: int32 [128], P('rp'), may hold values from 1 to 4
- electron_lattice: int32 [64, 3], replicated, may hold values from -6 to 6
- electron_degeneracy: int32 [64], replicated, may hold values from 1 to 6
- phonon_wavevectors: float32 [32, 3], replicated, may hold values from -0.5 to 0.5
- electron_wavevectors: float32 [256, 3], P('re'), may hold values from -0.5 to 0.5
- phonon_energies: float32 [32, 2], P('rp'), may hold values from 0.02 to 0.2
- bloch_rotations: float32 [256, 3200], P('re'), may hold values from -0.625 to 0.625
- band_energies: float32 [256, 40], P('re'), may hold values from -1.75 to 1.75
- shifted_points: int32 [32, 256], P('rp'), may hold values from 0 to 255, as said below
Outputs:
- linewidth: float32 [256, 40], P('re')
Inputs may be any that keep to these rules, and one draw needn't show every extreme that they name: `shifted_points`: row q gives, for every fine k-point k, the index of the fine k-point k+q, and is a permutation of the 256 points. Cut the points into blocks of 16 consecutive indices: for every q, the k+q points of one block lie in exactly 8 distinct blocks, exactly 2 in each.
All inputs are finite; a program needn't handle non-finite values.
Results may differ from a plain program's by a relative error of at most 0.0011.
Values may be sent and summed in bfloat16 or wider, within the bound.
A program may use at most 64 MiB of HBM per device.

v0:
```python
import math

import jax
import jax.numpy as jnp
from jax import lax
from jax.sharding import PartitionSpec as P

NW = 40
MODES = 2


full_turn = 2.0 * math.pi
thermal = 0.025
broadening = 0.05
highest = lax.Precision.HIGHEST


def phase_tables(points, lattice, degeneracy):
    angles = full_turn * jnp.dot(points, lattice.astype(jnp.float32).T, precision=highest)
    weights = 1.0 / degeneracy.astype(jnp.float32)
    return (
        (jnp.cos(angles) * weights).astype(jnp.bfloat16),
        (jnp.sin(angles) * weights).astype(jnp.bfloat16),
    )


def quarter_turn(flat_data):
    shaped = flat_data.reshape(flat_data.shape[:-1] + (MODES, 2, -1))
    turned = jnp.stack([-shaped[..., 1, :], shaped[..., 0, :]], axis=-2)
    return turned.reshape(flat_data.shape)


def lorentzian(offset):
    return broadening / math.pi / (offset * offset + broadening * broadening)


def coupling_strength(coupling, here_rotation, there_rotation):
    points = coupling.shape[0]
    shaped = coupling.reshape(points, MODES, 2, NW, NW)
    here_matrix = here_rotation.reshape(points, 2, NW, NW)
    there_matrix = there_rotation.reshape(points, 2, NW, NW)
    matrix_real = shaped[:, :, 0]
    matrix_imag = shaped[:, :, 1]
    right_real = here_matrix[:, 0]
    right_imag = here_matrix[:, 1]
    left_real = there_matrix[:, 0]
    left_imag = there_matrix[:, 1]
    mixed_real = jnp.einsum(
        "kmab,kbn->kman", matrix_real, right_real, precision=highest
    ) - jnp.einsum("kmab,kbn->kman", matrix_imag, right_imag, precision=highest)
    mixed_imag = jnp.einsum(
        "kmab,kbn->kman", matrix_real, right_imag, precision=highest
    ) + jnp.einsum("kmab,kbn->kman", matrix_imag, right_real, precision=highest)
    final_real = jnp.einsum(
        "kap,kman->kmpn", left_real, mixed_real, precision=highest
    ) + jnp.einsum("kap,kman->kmpn", left_imag, mixed_imag, precision=highest)
    final_imag = jnp.einsum(
        "kap,kman->kmpn", left_real, mixed_imag, precision=highest
    ) - jnp.einsum("kap,kman->kmpn", left_imag, mixed_real, precision=highest)
    return final_real * final_real + final_imag * final_imag


def scattering(strength, mode_energy, here_energy, there_energy):
    bose_factor = 1.0 / jnp.expm1(mode_energy / thermal)
    fermi_factor = jax.nn.sigmoid(-there_energy / thermal)
    phonon = mode_energy[None, :, None, None]
    occupied = bose_factor[None, :, None, None]
    filling = fermi_factor[:, None, :, None]
    spacing = here_energy[:, None, None, :] - there_energy[:, None, :, None]
    absorbed = (occupied + filling) * lorentzian(spacing + phonon)
    emitted = (occupied + 1.0 - filling) * lorentzian(spacing - phonon)
    return jnp.sum(strength / (2.0 * phonon) * (absorbed + emitted), axis=(1, 2))


def per_device(
    wannier_coupling,
    phonon_lattice,
    phonon_degeneracy,
    electron_lattice,
    electron_degeneracy,
    phonon_wavevectors,
    electron_wavevectors,
    phonon_energies,
    bloch_rotations,
    band_energies,
    shifted_points,
):
    point_count = bloch_rotations.shape[0]
    turned_local = quarter_turn(wannier_coupling)
    cosine_waves, sine_waves = phase_tables(phonon_wavevectors, phonon_lattice, phonon_degeneracy)
    summed_waves = lax.psum_scatter(
        jnp.einsum(
            "qr,erx->qex", cosine_waves, wannier_coupling, preferred_element_type=jnp.float32
        )
        + jnp.einsum("qr,erx->qex", sine_waves, turned_local, preferred_element_type=jnp.float32),
        "rp",
        scatter_dimension=0,
        tiled=True,
    )
    coupling_waves = summed_waves[0].astype(jnp.bfloat16)
    cosine_points, sine_points = phase_tables(
        electron_wavevectors, electron_lattice, electron_degeneracy
    )
    shard_rows = lax.all_gather(coupling_waves, "re", axis=0, tiled=True)
    coupling_points = jnp.dot(
        cosine_points, shard_rows, preferred_element_type=jnp.float32
    ) + jnp.dot(sine_points, quarter_turn(shard_rows), preferred_element_type=jnp.float32)
    wave_row = shifted_points[0]
    my_block = lax.axis_index("re")
    total_points = wave_row.shape[0]
    my_targets = lax.dynamic_slice_in_dim(wave_row, my_block * point_count, point_count)
    selector = (my_targets[:, None] == jnp.arange(total_points, dtype=jnp.int32)[None, :]).astype(
        jnp.float32
    )
    there_rotation = jnp.dot(
        selector, lax.all_gather(bloch_rotations, "re", axis=0, tiled=True), precision=highest
    )
    there_energy = jnp.dot(
        selector, lax.all_gather(band_energies, "re", axis=0, tiled=True), precision=highest
    )
    strength = coupling_strength(coupling_points, bloch_rotations, there_rotation)
    local_rates = scattering(strength, phonon_energies[0], band_energies, there_energy)
    total_rates = lax.psum(local_rates, "rp")
    return total_rates * (math.pi / (lax.axis_size("rp") * phonon_energies.shape[0]))


def solution(mesh):
    in_specs = (
        P("re", "rp", None),
        P("rp", None),
        P("rp"),
        P(),
        P(),
        P(),
        P("re", None),
        P("rp", None),
        P("re", None),
        P("re", None),
        P("rp", None),
    )
    out_specs = P("re", None)
    return jax.shard_map(
        per_device, mesh=mesh, in_specs=in_specs, out_specs=out_specs, check_vma=False
    )
```

profile of v0, /device:TPU:1, one launch (start us, length us, event | category | flops | bytes accessed | tf_op | source)
XLA Modules:
  0.0 401.8 jit_solution(2429475235229328539)
XLA Ops:
  6.6 0.7 all-gather.3.cloned.1.call-update
  7.3 0.7 convert_divide_fusion
  7.9 1.2 reshape.66
  9.1 0.5 slice_negate_fusion.1
  9.6 0.5 pad_maximum_fusion.1
  10.4 0.7 fusion.23
  11.1 0.7 convolution_add_fusion
  11.9 2.1 copy.22
  14.0 192.6 %all-reduce.2 = bf16[32,4,6400]{2,1,0:T(4,128)(2,1)} all-reduce(f32[32,4,6400]{2,1,0:T(4,128)S(1)} %copy.22), channel_id=3, replica_groups=mesh['rp'=32,'re'=16] {'rp'}, use_global_device_ids=true, to_apply=%region_0.0.clone | all-reduce | flops 819200 | bytes 4915200
  207.1 1.3 dynamic-slice.1
  208.3 1.5 dynamic-slice_convert_fusion
  209.9 45.3 %all-gather = bf16[1,64,6400]{2,0,1:T(2,128)(2,1)S(1)} all-gather(bf16[1,4,6400]{2,0,1:T(2,128)(2,1)S(1)} %copy.23), channel_id=2, replica_groups=mesh['rp'=32,'re'=16] {'re'}, dimensions={1}, use_global_device_ids=true | all-gather | bytes 870400 | tf_op jit(solution)/shard_map/all_gather | solution.py:104
  255.2 6.1 %reduce = bf16[64,6400]{1,0:T(8,128)(2,1)} reduce(bf16[1,64,6400]{2,0,1:T(2,128)(2,1)S(1)} %all-gather, bf16[]{:T(256)} %constant.44), dimensions={0}, to_apply=%all-gather.reduce_sub_computation | reduce | bytes 1638402 | tf_op jit(solution)/shard_map/all_gather | solution.py:104
  261.3 2.6 reshape.68
  263.9 1.9 slice_negate_fusion
  265.8 2.0 pad_maximum_fusion
  267.8 1.5 reshape.69
  269.8 0.6 copy-done.1
  270.7 1.1 reshape.70
  271.8 25.7 %all_gather.11 = f32[256,40]{1,0:T(8,128)S(1)} all-gather(f32[16,40]{1,0:T(8,128)S(1)} %copy-done.5), channel_id=1, replica_groups=mesh['rp'=32,'re'=16] {'re'}, dimensions={0}, use_global_device_ids=true | all-gather | bytes 43520 | tf_op jit(solution)/shard_map/all_gather | solution.py:119
  297.8 0.9 broadcast_subtract_fusion
  298.7 0.7 fusion.10
  299.4 0.7 fusion.11
  300.1 0.7 convolution_add_fusion.3
  300.9 0.7 convolution_subtract_fusion.1
  301.6 3.1 fusion.15
  305.2 0.8 fusion.12
  306.0 0.8 fusion.13
  306.8 0.8 fusion
  307.6 1.2 fusion.6
  308.7 85.6 %psum.7 = f32[16,40]{1,0:T(8,128)S(1)} all-reduce(f32[16,40]{1,0:T(8,128)S(1)} %fusion.6), channel_id=1, replica_groups=mesh['rp'=32,'re'=16] {'rp'}, use_global_device_ids=true, to_apply=%region_2.0 | all-reduce | flops 640 | bytes 5120 | tf_op jit(solution)/shard_map/psum | solution.py:123
  394.4 0.6 broadcast_multiply_fusion
  (38 shorter events, 2.5 us)
Async XLA Ops:
  6.5 262.7 %copy-start = (f32[16,3]{0,1:T(4,128)S(1)}, f32[16,3]{0,1:T(4,128)}, u32[]{:S(2)}) copy-start(f32[16,3]{0,1:T(4,128)} %param.17) | copy-start | bytes 580
  6.5 3.9 copy-start.2
  6.5 3.7 copy-start.7
  6.5 3.7 copy-start.6
  6.5 295.1 %all-gather.3.cloned.1.call-start = ((), (), s32[]{:S(2)}) async-start(), calls=%async_computation | async-start | bytes 3481600 | tf_op jit(solution)/shard_map/all_gather | solution.py:116
  14.0 192.6 %copy-start.3 = (f32[16,3200]{1,0:T(8,128)S(1)}, f32[16,3200]{1,0:T(8,128)}, u32[]{:S(2)}) copy-start(f32[16,3200]{1,0:T(8,128)} %param.19) | copy-start | bytes 614404
  265.8 3.5 copy-start.11
  265.8 3.5 copy-start.8
  269.3 1.1 copy-start.1
  270.4 1.3 copy-start.5
  270.4 27.0 %copy-start.10 = (s32[1,256]{1,0:T(1,128)S(1)}, s32[1,256]{1,0:T(1,128)}, u32[]{:S(2)}) copy-start(s32[1,256]{1,0:T(1,128)} %param.21) | copy-start | bytes 3076
  270.4 27.1 %copy-start.9 = (f32[1,2]{1,0:T(1,128)S(1)}, f32[1,2]{1,0:T(1,128)}, u32[]{:S(2)}) copy-start(f32[1,2]{1,0:T(1,128)} %param.18) | copy-start | bytes 28
  306.0 1.6 copy-start.4
Sparse Core Ops, SparseCore 0:
  9.5 116.5 all-gather.2
where the time goes:
time: 402 us
  blocking collectives  349 us (87%)
  between operations  13.7 us (3%)
  local copies, waits for them, and re-layouts  13.1 us (3%)
  other arithmetic  13.1 us (3%)
  matrix products  12 us (3%)
    unnamed x1, blocking collectives  193 us
    psum x1, blocking collectives, per_device(): total_rates = lax.psum(local_rates, 'rp')  85.6 us
    all_gather x1, blocking collectives, per_device(): shard_rows = lax.all_gather(coupling_waves, 're', axis=0, tiled=True)  45.3 us
    all_gather x1, blocking collectives, per_device(): lax.all_gather(band_energies, 're', axis=0, tiled=True)  25.7 us
  transfers between devices with their start and end apart: 1, of which 0 were waited for; matrix products, arithmetic and copies ran while one was open for 7% of the time, Pallas kernels for 0%

commit v1 on v0

v1 whole, which is shorter than its diff:
```python
import math

import jax
import jax.numpy as jnp
from jax import lax
from jax.experimental import pallas as pl
from jax.experimental.pallas import tpu as pltpu
from jax.sharding import PartitionSpec as P

NW = 40
MODES = 2
ROW = 1600
LANES = 1664
PACK = 512
MESH = pl.DeviceIdType.MESH
BF = jnp.bfloat16
F32 = jnp.float32

full_turn = 2.0 * math.pi
thermal = 0.025
broadening = 0.05
highest = lax.Precision.HIGHEST


def phase_tables(points, lattice, degeneracy):
    angles = full_turn * jnp.dot(points, lattice.astype(F32).T, precision=highest)
    weights = 1.0 / degeneracy.astype(F32)
    return (jnp.cos(angles) * weights).astype(BF), (jnp.sin(angles) * weights).astype(BF)


def three_parts(values):
    high = lax.reduce_precision(values, 8, 7)
    rest = values - high
    middle = lax.reduce_precision(rest, 8, 7)
    return high.astype(BF), middle.astype(BF), (rest - middle).astype(BF)


def iota(shape, axis):
    return lax.broadcasted_iota(jnp.int32, shape, axis)


def mm(left, right):
    return jnp.dot(left, right, preferred_element_type=F32)


def mm_first(left, right):
    return lax.dot_general(left, right, (((0,), (0,)), ((), ())), preferred_element_type=F32)


LANE_TILES = [(start, min(start + 256, LANES)) for start in range(0, LANES, 256)]


def kernel(
    w_ref,
    cosw_ref,
    sinw_ref,
    pack_ref,
    points_ref,
    phonon_ref,
    out_ref,
    w_sib,
    lhs_own,
    lhs_out,
    lhs_sib,
    packs,
    u_out,
    u_in,
    part,
    send_up,
    send_down,
    land_up,
    land_down,
    total,
    land_x,
    waves,
    mix,
    left_rot,
    right_rot,
    energy_col,
    energy_row,
    weight,
    coupling,
    rates,
    land_z,
    rates_z,
    land_c,
    core_s,
    core_r,
    pack_s,
    pack_r,
    u_s,
    u_r,
    up_s,
    up_r,
    down_s,
    down_r,
    x_s,
    x_r,
    yup_s,
    yup_r,
    ydown_s,
    ydown_r,
    rz_s,
    rz_r,
    rc_s,
    rc_r,
):
    rp = lax.axis_index("rp")
    re = lax.axis_index("re")
    z = rp // 4
    x_hi = (rp // 2) % 2
    core = rp % 2
    y = re // 2
    x_lo = re % 2

    def flip_rp(dx, dc):
        row = z * 4
        hi = (1 - x_hi) if dx else x_hi
        co = (1 - core) if dc else core
        return row + hi * 2 + co

    def flip_re(dl):
        return y * 2 + ((1 - x_lo) if dl else x_lo)

    def remote(src, dst, send, recv, to_rp, to_re):
        return pltpu.make_async_remote_copy(
            src_ref=src,
            dst_ref=dst,
            send_sem=send,
            recv_sem=recv,
            device_id={"rp": to_rp, "re": to_re},
            device_id_type=MESH,
        )

    partners = [(rp, (re + step) % 16) for step in range(1, 16)]
    partners += [((rp + 4 * step) % 32, re) for step in range(1, 8)]
    partners += [
        (flip_rp(dx, dc), flip_re(dl))
        for dx in (0, 1)
        for dc in (0, 1)
        for dl in (0, 1)
        if dx or dc
    ]
    barrier = pltpu.get_barrier_semaphore()
    for to_rp, to_re in partners:
        pl.semaphore_signal(
            barrier, inc=1, device_id={"rp": to_rp, "re": to_re}, device_id_type=MESH
        )

    row = iota((256, 128), 0)
    lane = iota((256, 128), 1)
    same = ((row >> 3) & 1 == (lane >> 5) & 1) & (row & 3 == (lane >> 2) & 3) & (lane < 64)
    to_imag = (row >> 2) & 1
    of_imag = (lane >> 4) & 1
    pick_cos = same & (to_imag == of_imag)
    pick_sin = same & (to_imag != of_imag)
    sign = jnp.where(to_imag == 1, 1.0, -1.0).astype(F32)
    q_row = iota((256, 32), 0)
    q_lane = iota((256, 32), 1)

    def phases_for(which_core):
        spread = jnp.where((q_row >> 4) * 2 + which_core == q_lane, 1.0, 0.0).astype(BF)
        cos_part = mm(spread, cosw_ref[...])
        sin_part = mm(spread, sinw_ref[...])
        return jnp.where(
            pick_cos, cos_part, jnp.where(pick_sin, sign * sin_part, 0.0)
        ).astype(BF)

    lhs_out[...] = phases_for(1 - core)

    points = points_ref[...]
    mine = (points >> 4) == re
    inner = points & 15
    smaller = jnp.min(jnp.where(mine, inner, 99), axis=1, keepdims=True)
    larger = jnp.max(jnp.where(mine, inner, -1), axis=1, keepdims=True)
    both = jnp.where(iota((16, 128), 1) == 0, smaller, larger).astype(F32).astype(BF)
    spread16 = jnp.where((iota((256, 16), 0) >> 4) == iota((256, 16), 1), 1.0, 0.0).astype(BF)
    both_rows = mm(spread16, both)
    slot = (iota((256, 1), 0) >> 3) & 1
    chosen = jnp.where(slot == 0, both_rows[:, 0:1], both_rows[:, 1:2])
    take = ((lane >> 3).astype(F32) == chosen) & ((lane & 7) == (row & 7))
    take = jnp.where(take, 1.0, 0.0).astype(BF)
    taken = mm(take, pack_ref[0:128, :]).astype(BF)
    u_out[...] = taken.reshape(8, 2, 16, PACK)

    pl.semaphore_wait(barrier, len(partners))

    sib = flip_rp(0, 1)
    core_copies = [
        remote(w_ref, w_sib, core_s.at[0], core_r.at[0], sib, re),
        remote(lhs_out, lhs_sib, core_s.at[1], core_r.at[1], sib, re),
    ]
    for copy in core_copies:
        copy.start()
    pack_copy = remote(pack_ref, packs.at[x_lo], pack_s, pack_r, rp, flip_re(1))
    pack_copy.start()
    u_copies = []
    for step in range(1, 16):
        to = (re + step) % 16
        copy = remote(
            u_out.at[to // 2], u_in.at[re], u_s.at[step], u_r.at[step], rp, to
        )
        copy.start()
        u_copies.append(copy)
    packs[x_lo] = pack_ref[...]
    u_in[re] = u_out[y]

    lhs_own[...] = phases_for(core)
    for start, end in LANE_TILES:
        part[:, start:end] = mm(lhs_own[:, 0:64], w_ref[:, start:end])
    for copy in core_copies:
        copy.wait_recv()
    for start, end in LANE_TILES:
        part[:, start:end] += mm(lhs_sib[:, 0:64], w_sib[:, start:end])

    above = (rp + 4) % 32
    below = (rp + 28) % 32

    def part_of(z_to, sub):
        hi = (1 - x_hi) if sub == 0 else x_hi
        block = (z_to % 8) * 2 + hi
        return part[pl.ds(pl.multiple_of(block * 16, 16), 16), :]

    sends = []

    def go_up(hop, sub):
        copy = remote(
            send_up.at[hop, sub],
            land_up.at[hop, sub],
            up_s.at[hop, sub],
            up_r.at[hop, sub],
            above,
            re,
        )
        copy.start()
        sends.append(copy)
        return copy

    def go_down(hop, sub):
        copy = remote(
            send_down.at[hop, sub],
            land_down.at[hop, sub],
            down_s.at[hop, sub],
            down_r.at[hop, sub],
            below,
            re,
        )
        copy.start()
        sends.append(copy)
        return copy

    ups = {}
    downs = {}
    for sub in (0, 1):
        send_up[0, sub] = part_of(z + 4, sub).astype(BF)
        ups[0, sub] = go_up(0, sub)
        send_down[0, sub] = part_of(z + 5, sub).astype(BF)
        downs[0, sub] = go_down(0, sub)

    def rotations_here():
        pack_copy.wait_recv()
        for b in (0, 1):
            rows = packs[b, 0:128, :].astype(F32)
            relayout(rows, right_rot, b, True)
            tail = packs[b, 128:144, :].astype(F32)
            energy_row[b * 16 : b * 16 + 16, :] = (
                tail[:, 128:256] + tail[:, 256:384] + tail[:, 384:512]
            )

    def relayout(rows, target, b, signed):
        swapped = jnp.concatenate(
            [rows.reshape(16, 8, PACK)[:, 4:8], rows.reshape(16, 8, PACK)[:, 0:4]], axis=1
        ).reshape(128, PACK)
        if signed:
            flip = jnp.where((iota((128, 1), 0) >> 2) & 1 == 1, -1.0, 1.0)
            rows = rows * flip
        for t in range(10):
            cut = slice(t * 40, t * 40 + 40)
            target[pl.ds(b * 1280 + t, 128, stride=10), :] = jnp.concatenate(
                [rows[:, cut], swapped[:, cut], jnp.zeros((128, 48), F32)], axis=1
            )

    def rotations_there():
        for copy in u_copies:
            copy.wait_recv()
        for b in (0, 1):
            block = points_ref[pl.ds(y * 2 + b, 1), :]
            spot = iota((128, 16), 0) >> 3 == iota((128, 16), 1)
            wide = jnp.broadcast_to(block, (128, 16))
            target = jnp.sum(jnp.where(spot, wide, 0), axis=1, keepdims=True)
            before = ((wide >> 4) == (target >> 4)) & (wide < target)
            second = jnp.max(jnp.where(before, 1, 0), axis=1, keepdims=True)
            source = (target >> 4) * 16 + second * 8 + (iota((128, 1), 0) & 7)
            order = jnp.where(iota((128, 256), 1) == source, 1.0, 0.0).astype(BF)
            rows = mm(order, u_in[:, b].reshape(256, PACK))
            relayout(rows, left_rot, b, False)
            for t in range(5):
                energy = (
                    rows[:, 400 + t : 401 + t]
                    + rows[:, 405 + t : 406 + t]
                    + rows[:, 410 + t : 411 + t]
                )
                energy_col[pl.ds(b * 640 + t, 128, stride=5), :] = jnp.broadcast_to(
                    energy, (128, 128)
                )

    def weights():
        omega = jnp.where(x_lo == 0, phonon_ref[0:1, 0:1], phonon_ref[0:1, 1:2])
        bose = 1.0 / (jnp.exp(omega / thermal) - 1.0)
        scale = (math.pi / 32.0) * (broadening / math.pi) / (2.0 * omega)

        def one(i, carry):
            there = energy_col[pl.ds(pl.multiple_of(i * 40, 8), 40), :]
            here = energy_row[pl.ds(i, 1), :]
            filling = 1.0 / (1.0 + jnp.exp(there / thermal))
            spacing = here - there
            plus = spacing + omega
            minus = spacing - omega
            wide = broadening * broadening
            weight[pl.ds(pl.multiple_of(i * 40, 8), 40), :] = scale * (
                (bose + filling) / (plus * plus + wide)
                + (bose + 1.0 - filling) / (minus * minus + wide)
            )
            return carry

        lax.fori_loop(0, 32, one, 0)

    def electron_phases():
        lane4 = iota((128, 128), 1)
        e_of_lane = ((lane4 >> 4) * 2 + (x_lo + ((lane4 >> 3) & 1)) % 2) * 4 + (lane4 & 3)
        row4 = iota((128, 128), 0)
        match = (row4 & 63) == e_of_lane
        sine = row4 >> 6
        imag = (lane4 >> 2) & 1
        to_real = jnp.where(match & (sine == imag), jnp.where(sine == 1, -1.0, 1.0), 0.0)
        to_im = jnp.where(match & (sine != imag), 1.0, 0.0)
        for b in (0, 1):
            table = packs[b, 128:144, 0:128]
            mix[b * 16 : b * 16 + 16, :] = mm(table, to_real.astype(BF)).astype(BF)
            mix[32 + b * 16 : 48 + b * 16, :] = mm(table, to_im.astype(BF)).astype(BF)

    rotations_here()

    for hop in (1, 2, 3):
        for sub in (0, 1):
            ups[hop - 1, sub].wait_recv()
            send_up[hop, sub] = (
                land_up[hop - 1, sub].astype(F32) + part_of(z + 4 - hop, sub)
            ).astype(BF)
            ups[hop, sub] = go_up(hop, sub)
            if hop < 3:
                downs[hop - 1, sub].wait_recv()
                send_down[hop, sub] = (
                    land_down[hop - 1, sub].astype(F32) + part_of(z + 5 + hop, sub)
                ).astype(BF)
                downs[hop, sub] = go_down(hop, sub)
        if hop == 1:
            electron_phases()
        if hop == 2:
            rotations_there()

    x_copies = {}
    for sub in (0, 1):
        ups[3, sub].wait_recv()
        downs[2, sub].wait_recv()
        done = (
            part_of(z, sub) + land_up[3, sub].astype(F32) + land_down[2, sub].astype(F32)
        )
        total[sub] = done.reshape(2, 8, LANES)
        for dl in (0, 1):
            if sub == 1 and dl == 0:
                continue
            dx = 1 - sub
            copy = remote(
                total.at[sub, (x_lo + dl) % 2],
                land_x.at[dx * 2 + dl],
                x_s.at[dx * 2 + dl],
                x_r.at[dx * 2 + dl],
                flip_rp(dx, 0),
                flip_re(dl),
            )
            copy.start()
            x_copies[dx, dl] = copy
    weights()
    for copy in x_copies.values():
        copy.wait_recv()
    near = total[1, x_lo] + land_x[2]
    far = land_x[1] + land_x[3]
    waves[y] = jnp.concatenate([near, far], axis=0).astype(BF)

    right = (re + 2) % 16
    left = (re + 14) % 16
    y_ups = []
    y_downs = []
    for hop in range(4):
        if hop > 0:
            y_ups[-1].wait_recv()
        block = (y + 8 - hop) % 8
        copy = remote(
            waves.at[block], waves.at[block], yup_s.at[hop], yup_r.at[hop], rp, right
        )
        copy.start()
        y_ups.append(copy)
        if hop < 3:
            if hop > 0:
                y_downs[-1].wait_recv()
            block = (y + hop) % 8
            copy = remote(
                waves.at[block], waves.at[block], ydown_s.at[hop], ydown_r.at[hop], rp, left
            )
            copy.start()
            y_downs.append(copy)
    y_ups[-1].wait_recv()
    y_downs[-1].wait_recv()

    everything = waves[...].reshape(128, LANES)
    points_c = mm(mix[...], everything)
    for a in range(40):
        cut = slice(a * 40, a * 40 + 40)
        coupling[pl.ds(a, 32, stride=40), :] = jnp.concatenate(
            [points_c[0:32, cut], points_c[32:64, cut], jnp.zeros((32, 48), F32)], axis=1
        )

    def one_point(i, carry):
        here = right_rot[pl.ds(pl.multiple_of(i * 80, 8), 80), 0:80].astype(BF)
        there = left_rot[pl.ds(pl.multiple_of(i * 80, 8), 40), 0:80].astype(BF)
        block = coupling[pl.ds(pl.multiple_of(i * 40, 8), 40), 0:80].astype(BF)
        mixed = mm(block, here).astype(BF)
        final = mm_first(there, mixed)
        real = final[0:40, 0:40] + final[40:80, 40:80]
        imag = final[0:40, 40:80] - final[40:80, 0:40]
        strength = real * real + imag * imag
        terms = strength * weight[pl.ds(pl.multiple_of(i * 40, 8), 40), 0:40]
        rates[pl.ds(i, 1), 0:40] = jnp.sum(terms, axis=0, keepdims=True)
        return carry

    rates[...] = jnp.zeros((32, 128), F32)
    lax.fori_loop(0, 32, one_point, 0)

    z_copies = []
    for step in range(1, 8):
        copy = remote(
            rates, land_z.at[step - 1], rz_s.at[step], rz_r.at[step], (rp + 4 * step) % 32, re
        )
        copy.start()
        z_copies.append(copy)
    summed = rates[...]
    for step in range(1, 8):
        z_copies[step - 1].wait_recv()
        summed = summed + land_z[step - 1]
    rates_z[...] = summed.reshape(2, 16, 128)
    c_copies = []
    for dx in (0, 1):
        for dc in (0, 1):
            for dl in (0, 1):
                slot_c = dx * 4 + dc * 2 + dl
                if slot_c == 0:
                    continue
                copy = remote(
                    rates_z.at[(x_lo + dl) % 2],
                    land_c.at[slot_c],
                    rc_s.at[slot_c],
                    rc_r.at[slot_c],
                    flip_rp(dx, dc),
                    flip_re(dl),
                )
                copy.start()
                c_copies.append((slot_c, copy))
    final_sum = rates_z[x_lo]
    for slot_c, copy in c_copies:
        copy.wait_recv()
        final_sum = final_sum + land_c[slot_c]
    out_ref[...] = final_sum[:, 0:40]

    for copy in core_copies + [pack_copy] + u_copies + sends + list(x_copies.values()):
        copy.wait_send()
    for copy in y_ups + y_downs + z_copies:
        copy.wait_send()
    for _, copy in c_copies:
        copy.wait_send()


def per_device(
    wannier_coupling,
    phonon_lattice,
    phonon_degeneracy,
    electron_lattice,
    electron_degeneracy,
    phonon_wavevectors,
    electron_wavevectors,
    phonon_energies,
    bloch_rotations,
    band_energies,
    shifted_points,
):
    w = wannier_coupling.reshape(16, 4, ROW).transpose(1, 0, 2).reshape(64, ROW)
    w = jnp.pad(w, ((0, 0), (0, LANES - ROW)))
    cosw, sinw = phase_tables(
        phonon_wavevectors, jnp.tile(phonon_lattice, (32, 1)), jnp.tile(phonon_degeneracy, 32)
    )
    cosk, sink = phase_tables(electron_wavevectors, electron_lattice, electron_degeneracy)
    energies = [part.reshape(128, 5) for part in three_parts(band_energies)]
    upper = jnp.concatenate(
        [bloch_rotations.reshape(128, 400).astype(BF)] + energies + [jnp.zeros((128, 97), BF)],
        axis=1,
    )
    lower = [cosk, sink]
    for part in three_parts(band_energies):
        lower += [part, jnp.zeros((16, 88), BF)]
    pack = jnp.concatenate([upper, jnp.concatenate(lower, axis=1)], axis=0)
    points = shifted_points.reshape(16, 16)

    def vm(shape, dtype):
        return pltpu.VMEM(shape, dtype)

    dma = pltpu.SemaphoreType.DMA
    return pl.pallas_call(
        kernel,
        out_shape=jax.ShapeDtypeStruct((16, 40), F32),
        in_specs=[pl.BlockSpec(memory_space=pltpu.VMEM)] * 6,
        out_specs=pl.BlockSpec(memory_space=pltpu.VMEM),
        scratch_shapes=[
            vm((64, LANES), BF),
            vm((256, 128), BF),
            vm((256, 128), BF),
            vm((256, 128), BF),
            vm((2, 144, PACK), BF),
            vm((8, 2, 16, PACK), BF),
            vm((16, 2, 16, PACK), BF),
            vm((256, LANES), F32),
            vm((4, 2, 16, LANES), BF),
            vm((3, 2, 16, LANES), BF),
            vm((4, 2, 16, LANES), BF),
            vm((3, 2, 16, LANES), BF),
            vm((2, 2, 8, LANES), F32),
            vm((4, 8, LANES), F32),
            vm((8, 16, LANES), BF),
            vm((64, 128), BF),
            vm((2560, 128), F32),
            vm((2560, 128), F32),
            vm((1280, 128), F32),
            vm((32, 128), F32),
            vm((1280, 128), F32),
            vm((1280, 128), F32),
            vm((32, 128), F32),
            vm((7, 32, 128), F32),
            vm((2, 16, 128), F32),
            vm((8, 16, 128), F32),
            dma((2,)),
            dma((2,)),
            dma,
            dma,
            dma((16,)),
            dma((16,)),
            dma((4, 2)),
            dma((4, 2)),
            dma((3, 2)),
            dma((3, 2)),
            dma((4,)),
            dma((4,)),
            dma((4,)),
            dma((4,)),
            dma((3,)),
            dma((3,)),
            dma((8,)),
            dma((8,)),
            dma((8,)),
            dma((8,)),
        ],
        compiler_params=pltpu.CompilerParams(
            collective_id=0, has_side_effects=True, vmem_limit_bytes=40 * 1024 * 1024
        ),
        cost_estimate=pl.CostEstimate(
            flops=300_000_000, bytes_accessed=2_000_000, transcendentals=200_000
        ),
    )(w, cosw, sinw, pack, points, phonon_energies)


def solution(mesh):
    in_specs = (
        P("re", "rp", None),
        P("rp", None),
        P("rp"),
        P(),
        P(),
        P(),
        P("re", None),
        P("rp", None),
        P("re", None),
        P("re", None),
        P("rp", None),
    )
    return jax.shard_map(
        per_device, mesh=mesh, in_specs=in_specs, out_specs=P("re", None), check_vma=False
    )
```

time: 402 us -> 85.5 us (0.21)
  blocking collectives: 349 us -> 0 us
  Pallas kernels: 0 us -> 77.3 us
  between operations: 13.7 us -> 0.18 us
  other arithmetic: 13.1 us -> 2.1 us
  matrix products: 12 us -> 1.3 us
  local copies, waits for them, and re-layouts: 13.1 us -> 4.42 us
    unnamed x1 -> x0, blocking collectives: 193 us -> none
    psum x1 -> x0, blocking collectives: 85.6 us -> none  [per_device(): total_rates = lax.psum(local_rates, 'rp')]
    pallas_call x0 -> x1, Pallas kernels: none -> 77.3 us  [per_device(): pl.pallas_call(kernel, out_shape=jax.ShapeDtypeStruct((16, 40), F32), in_...]
    all_gather x2 -> x0, blocking collectives: 71 us -> none  [the longest x1 45.3 us: per_device(): shard_rows = lax.all_gather(coupling_waves, 're', axis=0, tiled=True)]
    dot_general x16 -> x2, matrix products: 12 us -> 1.3 us  [phase_tables(): jnp.dot(points, lattice.astype(F32).T, precision=highest)]
    reshape x7 -> x6, local copies, waits for them, and re-layouts: 7.44 us -> 0.62 us  [the longest x2 0.29 us: per_device(): w = wannier_coupling.reshape(16, 4, ROW).transpose(1, 0, 2).reshape(64, ROW)]
    all_gather x1 -> x0, other arithmetic: 6.06 us -> none  [per_device(): shard_rows = lax.all_gather(coupling_waves, 're', axis=0, tiled=True)]
  transfers between devices with their start and end apart: 1 -> 0, of which waited for: 0 -> 0; matrix products, arithmetic and copies ran while one was open for 7% -> 0% of each run, Pallas kernels for 0% -> 0%
where the time goes in v1:
time: 85.5 us; the launch traced here: 85.2 us
  Pallas kernels  77.3 us (90%)
  local copies, waits for them, and re-layouts  4.42 us (5%)
  other arithmetic  2.1 us (2%)
  matrix products  1.3 us (2%)
    pallas_call x1, Pallas kernels, per_device(): pl.pallas_call(kernel, out_shape=jax.ShapeDtypeStruct((16, 40), F32), in_...  77.3 us
    unnamed x16, local copies, waits for them, and re-layouts  3.15 us

profile of v1, /device:TPU:1, one launch (start us, length us, event | category | flops | bytes accessed | tf_op | source)
XLA Modules:
  0.0 85.2 jit_solution(1742158508712207515)
XLA Ops:
  0.0 0.0 copy-start
  0.0 0.0 copy-start.2
  0.0 0.7 fusion
  0.7 0.7 convert_divide_fusion
  1.4 1.0 %multiply_convert_fusion.2 = (bf16[16,64]{1,0:T(8,128)(2,1)S(1)}, bf16[16,64]{1,0:T(8,128)(2,1)S(1)}) fusion(f32[64]{0:T(128)S(1)} %convert_divide_fusion, f32[16,3]{0,1:T(4,128)} %param.17, s32[64,3]{0,1:T(4,128)} %param.14), kind=kOutput, calls=%fused_computation.10 | convolution fusion | flops 42176 | bytes 5312 | tf_op jit(solution)/shard_map/dot_general | solution.py:26
  2.4 0.1 concatenate.10
  2.5 0.1 reshape.38
  2.6 0.1 reshape.39
  2.6 0.1 reshape.40
  2.7 0.0 copy-done.2
  2.8 0.3 convert_element_type.60
  3.1 0.1 concatenate.9
  3.2 0.0 copy-start.4
  3.2 0.0 copy-start.3
  3.2 0.6 copy-done.4
  3.9 0.0 copy-start.6
  3.9 0.6 copy-done.6
  4.6 0.1 div.22
  4.7 0.0 copy-done
  4.7 0.3 multiply_convert_fusion
  5.0 0.0 copy-done.3
  5.0 0.3 reshape.36
  5.4 0.0 copy-start.5
  5.4 0.5 broadcast.24
  5.9 0.2 copy-done.5
  6.1 0.7 reduce.3
  6.7 0.0 copy-start.1
  6.7 0.1 reshape.41.points_ref
  6.8 0.6 copy-done.1
  7.4 77.3 %shard_map.109 = f32[16,40]{1,0:T(8,128)S(1)} custom-call(bf16[64,1664]{1,0:T(8,128)(2,1)S(1)} %pad.4.w_ref, bf16[32,128]{1,0:T(8,128)(2,1)S(1)} %get-tuple-element.6.cosw_ref, bf16[32,128]{1,0:T(8,128)(2,1)S(1)} %get-tuple-element.5.sinw_ref, bf16[144,512]{1,0:T(8,128)(2,1)S(1)} %pad_maximum_fusion.pack_ref, s32[16,16]{1,0:T(8,128)S(1)} %reshape.41.points_ref, ...), custom_call_target="tpu_custom_call" | custom-call | flops 300000000 | bytes 2000000 | tf_op jit(solution)/shard_map/pallas_call | solution.py:517
  84.6 0.6 copy.15
  (10 shorter events, 0.1 us)
Async XLA Ops:
  0.0 4.7 %copy-start = (f32[32,3]{0,1:T(4,128)S(1)}, f32[32,3]{0,1:T(4,128)}, u32[]{:S(2)}) copy-start(f32[32,3]{0,1:T(4,128)} %param.16) | copy-start | bytes 1156
  0.0 2.7 %copy-start.2 = (f32[16,3200]{1,0:T(8,128)S(1)}, f32[16,3200]{1,0:T(8,128)}, u32[]{:S(2)}) copy-start(f32[16,3200]{1,0:T(8,128)} %param.19) | copy-start | bytes 614404
  3.2 0.7 copy-start.4
  3.2 1.8 %copy-start.3 = (bf16[4,4,6400]{2,1,0:T(4,128)(2,1)S(1)}, bf16[4,4,6400]{2,1,0:T(4,128)(2,1)}, u32[]{:S(2)}) copy-start(bf16[4,4,6400]{2,1,0:T(4,128)(2,1)} %param.11) | copy-start | bytes 614404
  3.9 0.7 copy-start.6
  5.4 0.7 copy-start.5
  6.7 0.7 copy-start.1

commit v2 on v1

v2 whole, which is shorter than its diff:
```python
import math

import jax
import jax.numpy as jnp
from jax import lax
from jax.experimental import pallas as pl
from jax.experimental.pallas import tpu as pltpu
from jax.sharding import PartitionSpec as P

NW = 40
MODES = 2
ROW = 1600
LANES = 1664
PACK = 512
MESH = pl.DeviceIdType.MESH
BF = jnp.bfloat16
F32 = jnp.float32

full_turn = 2.0 * math.pi
thermal = 0.025
broadening = 0.05
highest = lax.Precision.HIGHEST


def three_parts(values):
    high = values.astype(BF).astype(F32)
    rest = values - high
    middle = rest.astype(BF).astype(F32)
    return high, middle, rest - middle


def iota(shape, axis):
    return lax.broadcasted_iota(jnp.int32, shape, axis)


def mm(left, right):
    return jnp.dot(left, right, preferred_element_type=F32)


def outer(left, right):
    return lax.dot_general(
        left, right, (((0,), (0,)), ((), ())), precision=highest, preferred_element_type=F32
    )


LANE_TILES = [(start, min(start + 256, LANES)) for start in range(0, LANES, 256)]
HALF = 896


def kernel(
    w_ref,
    plat_ref,
    pdeg_ref,
    elat_ref,
    edeg_ref,
    qvec_ref,
    kvec_ref,
    phonon_ref,
    rot_ref,
    band_ref,
    shift_ref,
    out_ref,
    w_own,
    w_sib,
    cosw,
    sinw,
    lhs_own,
    lhs_out,
    lhs_sib,
    points_ref,
    pack_f,
    pack,
    packs,
    u_out,
    u_in,
    part,
    s_far,
    l_far,
    s_opp,
    l_opp,
    s_near,
    l_near,
    s_two,
    l_two,
    total,
    land_x,
    waves,
    mix,
    turn_a,
    turn_b,
    right_rot,
    left_rot,
    energy_col,
    energy_row,
    weight,
    coupling,
    rates,
    rates_b,
    land_c,
    rates_z,
    land_z,
    core_s,
    core_r,
    pack_s,
    pack_r,
    u_s,
    u_r,
    far_s,
    far_r,
    opp_s,
    opp_r,
    near_s,
    near_r,
    two_s,
    two_r,
    x_s,
    x_r,
    y1_s,
    y1_r,
    y2_s,
    y2_r,
    rc_s,
    rc_r,
    rz_s,
    rz_r,
):
    rp = lax.axis_index("rp")
    re = lax.axis_index("re")
    z = rp // 4
    x_hi = (rp // 2) % 2
    core = rp % 2
    y = re // 2
    x_lo = re % 2

    def flip_rp(dx, dc):
        hi = (1 - x_hi) if dx else x_hi
        co = (1 - core) if dc else core
        return z * 4 + hi * 2 + co

    def flip_re(dl):
        return y * 2 + ((1 - x_lo) if dl else x_lo)

    def along_z(step):
        return (rp + 32 + 4 * step) % 32

    def along_y(step):
        return (re + 16 + 2 * step) % 16

    started = []

    def remote(src, dst, send, recv, to_rp, to_re):
        copy = pltpu.make_async_remote_copy(
            src_ref=src,
            dst_ref=dst,
            send_sem=send,
            recv_sem=recv,
            device_id={"rp": to_rp, "re": to_re},
            device_id_type=MESH,
        )
        copy.start()
        started.append(copy)
        return copy

    partners = [(rp, (re + step) % 16) for step in range(1, 16)]
    partners += [(along_z(step), re) for step in range(1, 8)]
    partners += [
        (flip_rp(dx, dc), flip_re(dl))
        for dx in (0, 1)
        for dc in (0, 1)
        for dl in (0, 1)
        if dx or dc
    ]
    barrier = pltpu.get_barrier_semaphore()
    for to_rp, to_re in partners:
        pl.semaphore_signal(
            barrier, inc=1, device_id={"rp": to_rp, "re": to_re}, device_id_type=MESH
        )

    cells = jnp.concatenate([w_ref[e].astype(F32) for e in range(4)], axis=0)
    for mc in range(4):
        w_own[mc * 16 : mc * 16 + 16, :] = jnp.concatenate(
            [cells[:, mc * ROW : (mc + 1) * ROW], jnp.zeros((16, LANES - ROW), F32)], axis=1
        ).astype(BF)

    r_of_lane = jnp.where(iota((4, 128), 0) == (iota((4, 128), 1) & 3), 1.0, 0.0).astype(F32)
    p_angle = full_turn * outer(qvec_ref[...], outer(plat_ref[...].astype(F32), r_of_lane))
    p_weight = 1.0 / outer(pdeg_ref[...].astype(F32), r_of_lane)
    cosw[...] = (jnp.cos(p_angle) * p_weight).astype(BF)
    sinw[...] = (jnp.sin(p_angle) * p_weight).astype(BF)
    row = iota((256, 128), 0)
    lane = iota((256, 128), 1)
    same = ((row >> 3) & 1 == (lane >> 5) & 1) & (row & 3 == (lane >> 2) & 3) & (lane < 64)
    to_imag = (row >> 2) & 1
    of_imag = (lane >> 4) & 1
    pick_cos = same & (to_imag == of_imag)
    pick_sin = same & (to_imag != of_imag)
    sign = jnp.where(to_imag == 1, 1.0, -1.0).astype(F32)
    q_row = iota((256, 32), 0)
    q_lane = iota((256, 32), 1)

    def phases_for(which_core):
        spread = jnp.where((q_row >> 4) * 2 + which_core == q_lane, 1.0, 0.0).astype(BF)
        cos_part = mm(spread, cosw[...])
        sin_part = mm(spread, sinw[...])
        return jnp.where(
            pick_cos, cos_part, jnp.where(pick_sin, sign * sin_part, 0.0)
        ).astype(BF)

    lhs_out[...] = phases_for(1 - core)

    pl.semaphore_wait(barrier, len(partners))

    sib = flip_rp(0, 1)
    core_copies = [
        remote(w_own, w_sib, core_s.at[0], core_r.at[0], sib, re),
        remote(lhs_out, lhs_sib, core_s.at[1], core_r.at[1], sib, re),
    ]

    lhs_own[...] = phases_for(core)
    for start, end in LANE_TILES:
        part[:, start:end] = mm(lhs_own[:, 0:64], w_own[:, start:end])
    for copy in core_copies:
        copy.wait_recv()
    for start, end in LANE_TILES:
        part[:, start:end] += mm(lhs_sib[:, 0:64], w_sib[:, start:end])

    def part_of(z_to, sub):
        hi = (1 - x_hi) if sub == 0 else x_hi
        block = ((z_to + 8) % 8) * 2 + hi
        return part[pl.ds(pl.multiple_of(block * 16, 16), 16), :]

    far = {}
    opp = {}
    for sub in (0, 1):
        toward = 2 if sub == 0 else -2
        s_opp[sub] = part_of(z + 4, sub).astype(BF)
        opp[sub] = remote(
            s_opp.at[sub], l_opp.at[sub], opp_s.at[sub], opp_r.at[sub], along_z(toward), re
        )
        for side, step in ((0, 1), (1, -1)):
            s_far[side, sub] = part_of(z + 3 * step, sub).astype(BF)
            far[side, sub] = remote(
                s_far.at[side, sub],
                l_far.at[side, sub],
                far_s.at[side, sub],
                far_r.at[side, sub],
                along_z(step),
                re,
            )
    near = {}
    for side, step in ((0, 1), (1, -1)):
        for sub in (0, 1):
            s_near[side, sub] = part_of(z + step, sub).astype(BF)
        near[side] = remote(
            s_near.at[side], l_near.at[side], near_s.at[side], near_r.at[side], along_z(step), re
        )

    e_angle = full_turn * outer(kvec_ref[...], elat_ref[...].astype(F32))
    e_weight = 1.0 / edeg_ref[...].astype(F32)
    high, middle, low = three_parts(band_ref[...])
    gap = jnp.zeros((16, 48), F32)
    pack[128:144, :] = jnp.concatenate(
        [jnp.cos(e_angle) * e_weight, jnp.sin(e_angle) * e_weight]
        + [high, high, gap, middle, middle, gap, low, low, gap],
        axis=1,
    ).astype(BF)
    rest = jnp.zeros((16, PACK - 415), F32)
    for j in range(8):
        five = slice(j * 5, j * 5 + 5)
        eighth = jnp.concatenate(
            [rot_ref[:, j * 400 : j * 400 + 400], high[:, five], middle[:, five], low[:, five], rest],
            axis=1,
        )
        for v in range(4):
            pack_f[v, pl.ds(j, 16, stride=8), :] = eighth[:, v * 128 : v * 128 + 128]
    for v in range(4):
        pack[0:128, v * 128 : v * 128 + 128] = pack_f[v].astype(BF)
    pack_copy = remote(pack, packs.at[x_lo], pack_s, pack_r, rp, flip_re(1))

    for d in range(16):
        points_ref[d : d + 1, :] = shift_ref[:, d * 16 : d * 16 + 16]
    points = points_ref[...]
    mine = (points >> 4) == re
    inner = points & 15
    smaller = jnp.min(jnp.where(mine, inner, 99), axis=1, keepdims=True)
    larger = jnp.max(jnp.where(mine, inner, -1), axis=1, keepdims=True)
    both = jnp.where(iota((16, 128), 1) == 0, smaller, larger).astype(F32).astype(BF)
    spread16 = jnp.where((iota((256, 16), 0) >> 4) == iota((256, 16), 1), 1.0, 0.0).astype(BF)
    both_rows = mm(spread16, both)
    slot = (iota((256, 1), 0) >> 3) & 1
    chosen = jnp.where(slot == 0, both_rows[:, 0:1], both_rows[:, 1:2])
    take = ((lane >> 3).astype(F32) == chosen) & ((lane & 7) == (row & 7))
    take = jnp.where(take, 1.0, 0.0).astype(BF)
    u_out[...] = mm(take, pack[0:128, :]).astype(BF).reshape(8, 2, 16, PACK)
    u_copies = []
    for step in range(1, 16):
        to = (re + step) % 16
        u_copies.append(
            remote(u_out.at[to // 2], u_in.at[re], u_s.at[step], u_r.at[step], rp, to)
        )
    packs[x_lo] = pack[...]
    u_in[re] = u_out[y]

    two = {}
    for sub in (0, 1):
        for side, step in ((0, 1), (1, -1)):
            far[side, sub].wait_recv()
            done = part_of(z + 2 * step, sub) + l_far[side, sub].astype(F32)
            if side == sub:
                opp[sub].wait_recv()
                done = done + l_opp[sub].astype(F32)
            s_two[side, sub] = done.astype(BF)
            two[side, sub] = remote(
                s_two.at[side, sub],
                l_two.at[side, sub],
                two_s.at[side, sub],
                two_r.at[side, sub],
                along_z(2 * step),
                re,
            )

    def swap_halves(rows):
        cut = rows.reshape(16, 8, PACK)
        return jnp.concatenate([cut[:, 4:8], cut[:, 0:4]], axis=1).reshape(128, PACK)

    def rotations_here():
        pack_copy.wait_recv()
        blank = jnp.zeros((128, 48), F32)
        for b in (0, 1):
            rows = packs[b, 0:128, :].astype(F32)
            swapped = swap_halves(rows)
            rows = rows * jnp.where((iota((128, 1), 0) >> 2) & 1 == 1, -1.0, 1.0)
            for t in range(10):
                cut = slice(t * 40, t * 40 + 40)
                spot = pl.ds(b * 1280 + t, 128, stride=10)
                turn_a[spot, :] = jnp.concatenate([rows[:, cut], swapped[:, cut], blank], axis=1)
                turn_b[spot, :] = jnp.concatenate([swapped[:, cut], -rows[:, cut], blank], axis=1)
            tail = packs[b, 128:144, :].astype(F32)
            energy_row[b * 16 : b * 16 + 16, :] = (
                tail[:, 128:256] + tail[:, 256:384] + tail[:, 384:512]
            )

        def one(i, carry):
            spot = pl.ds(pl.multiple_of(i * 80, 8), 80)
            right_rot[i] = jnp.concatenate([turn_a[spot, :], turn_b[spot, :]], axis=1).astype(BF)
            return carry

        lax.fori_loop(0, 32, one, 0)

    def rotations_there():
        for copy in u_copies:
            copy.wait_recv()
        blank = jnp.zeros((128, 88), F32)
        for b in (0, 1):
            block = points_ref[pl.ds(y * 2 + b, 1), :]
            spot = iota((128, 16), 0) >> 3 == iota((128, 16), 1)
            wide = jnp.broadcast_to(block, (128, 16))
            target = jnp.sum(jnp.where(spot, wide, 0), axis=1, keepdims=True)
            before = ((wide >> 4) == (target >> 4)) & (wide < target)
            second = jnp.max(jnp.where(before, 1, 0), axis=1, keepdims=True)
            source = (target >> 4) * 16 + second * 8 + (iota((128, 1), 0) & 7)
            order = jnp.where(iota((128, 256), 1) == source, 1.0, 0.0).astype(BF)
            rows = mm(order, u_in[:, b].reshape(256, PACK))
            for t in range(10):
                turn_a[pl.ds(b * 1280 + t, 128, stride=10), :] = jnp.concatenate(
                    [rows[:, t * 40 : t * 40 + 40], blank], axis=1
                )
            for t in range(5):
                energy = (
                    rows[:, 400 + t : 401 + t]
                    + rows[:, 405 + t : 406 + t]
                    + rows[:, 410 + t : 411 + t]
                )
                energy_col[pl.ds(b * 640 + t, 128, stride=5), :] = jnp.broadcast_to(
                    energy, (128, 128)
                )

        def one(i, carry):
            spot = pl.ds(pl.multiple_of(i * 80, 8), 80)
            left_rot[i, :, 0:80] = jnp.transpose(turn_a[spot, :])[0:48, :].astype(BF)
            return carry

        lax.fori_loop(0, 32, one, 0)

    def weights():
        omega = jnp.where(x_lo == 0, phonon_ref[0:1, 0:1], phonon_ref[0:1, 1:2])
        bose = 1.0 / (jnp.exp(omega / thermal) - 1.0)
        scale = (math.pi / 32.0) * (broadening / math.pi) / (2.0 * omega)

        def one(i, carry):
            there = energy_col[pl.ds(pl.multiple_of(i * 40, 8), 40), :]
            here = energy_row[pl.ds(i, 1), :]
            filling = 1.0 / (1.0 + jnp.exp(there / thermal))
            spacing = here - there
            plus = spacing + omega
            minus = spacing - omega
            wide = broadening * broadening
            weight[pl.ds(pl.multiple_of(i * 40, 8), 40), :] = scale * (
                (bose + filling) / (plus * plus + wide)
                + (bose + 1.0 - filling) / (minus * minus + wide)
            )
            return carry

        lax.fori_loop(0, 32, one, 0)

    def electron_phases():
        lane4 = iota((128, 128), 1)
        place = lane4 >> 4
        ahead = (place + 1) >> 1
        source = (y + 8 + jnp.where(place & 1 == 1, ahead, -ahead)) & 7
        e_of_lane = (source * 2 + ((x_lo + (lane4 >> 3)) & 1)) * 4 + (lane4 & 3)
        row4 = iota((128, 128), 0)
        match = (row4 & 63) == e_of_lane
        sine = row4 >> 6
        imag = (lane4 >> 2) & 1
        to_real = jnp.where(match & (sine == imag), jnp.where(sine == 1, -1.0, 1.0), 0.0)
        to_im = jnp.where(match & (sine != imag), 1.0, 0.0)
        for b in (0, 1):
            table = packs[b, 128:144, 0:128]
            mix[b * 16 : b * 16 + 16, :] = mm(table, to_real.astype(BF)).astype(BF)
            mix[32 + b * 16 : 48 + b * 16, :] = mm(table, to_im.astype(BF)).astype(BF)

    rotations_here()
    electron_phases()

    x_copies = {}
    for side in (0, 1):
        near[side].wait_recv()
    for sub in (0, 1):
        done = part_of(z, sub) + l_near[0, sub].astype(F32) + l_near[1, sub].astype(F32)
        for side in (0, 1):
            two[side, sub].wait_recv()
            done = done + l_two[side, sub].astype(F32)
        total[sub] = done.reshape(2, 8, LANES)
        for dl in (0, 1):
            if sub == 1 and dl == 0:
                continue
            dx = 1 - sub
            spot = dx * 2 + dl
            x_copies[spot] = remote(
                total.at[sub, (x_lo + dl) % 2],
                land_x.at[spot],
                x_s.at[spot],
                x_r.at[spot],
                flip_rp(dx, 0),
                flip_re(dl),
            )
    rotations_there()
    for copy in x_copies.values():
        copy.wait_recv()
    waves[0] = jnp.concatenate(
        [total[1, x_lo] + land_x[2], land_x[1] + land_x[3]], axis=0
    ).astype(BF)

    first = {}
    for place, step in ((4, 2), (3, -2), (2, 1), (1, -1)):
        first[place] = remote(
            waves.at[0], waves.at[place], y1_s.at[place], y1_r.at[place], rp, along_y(step)
        )
    weights()
    first[2].wait_recv()
    later = [remote(waves.at[2], waves.at[6], y2_s.at[0], y2_r.at[0], rp, along_y(2))]
    first[1].wait_recv()
    later.append(remote(waves.at[1], waves.at[5], y2_s.at[1], y2_r.at[1], rp, along_y(-2)))
    lower = pl.ds(0, HALF)
    upper = pl.ds(HALF, LANES - HALF)
    first[4].wait_recv()
    later.append(
        remote(
            waves.at[4, :, lower],
            waves.at[7, :, lower],
            y2_s.at[2],
            y2_r.at[2],
            rp,
            along_y(2),
        )
    )
    first[3].wait_recv()
    later.append(
        remote(
            waves.at[3, :, upper],
            waves.at[7, :, upper],
            y2_s.at[3],
            y2_r.at[3],
            rp,
            along_y(-2),
        )
    )
    points_c = mm(mix[:, 0:80], waves[0:5].reshape(80, LANES))
    for copy in later:
        copy.wait_recv()
    points_c = points_c + mm(mix[:, 80:128], waves[5:8].reshape(48, LANES))

    for a in range(40):
        cut = slice(a * 40, a * 40 + 40)
        coupling[pl.ds(a, 32, stride=40), :] = jnp.concatenate(
            [points_c[0:32, cut], points_c[32:64, cut], jnp.zeros((32, 48), F32)], axis=1
        )

    def some_points(group, carry):
        indices = [group * 8 + i for i in range(8)]
        spots = [pl.ds(pl.multiple_of(i * 40, 8), 40) for i in indices]
        turned = [
            mm(coupling[spot, 0:80].astype(BF), right_rot[i])
            for i, spot in zip(indices, spots, strict=True)
        ]
        stacked = [
            jnp.concatenate([t[:, 0:80], t[:, 128:208]], axis=0).astype(BF) for t in turned
        ]
        final = [
            mm(left_rot[i, 0:40, 0:80], s) for i, s in zip(indices, stacked, strict=True)
        ]
        sums = [
            jnp.sum(f * f * weight[spot, 0:80], axis=0, keepdims=True)
            for f, spot in zip(final, spots, strict=True)
        ]
        rates[pl.ds(pl.multiple_of(group * 8, 8), 8), 0:80] = jnp.concatenate(sums, axis=0)
        return carry

    lax.fori_loop(0, 4, some_points, 0)

    for b in (0, 1):
        rows = rates[b * 16 : b * 16 + 16, 0:40] + rates[b * 16 : b * 16 + 16, 40:80]
        rates_b[b] = jnp.concatenate([rows[0:8], rows[8:16], jnp.zeros((8, 48), F32)], axis=1)
    c_copies = []
    for dx in (1, 0):
        for dl in (1, 0):
            for dc in (1, 0):
                spot = dx * 4 + dc * 2 + dl
                if spot == 0:
                    continue
                copy = remote(
                    rates_b.at[(x_lo + dl) % 2],
                    land_c.at[spot],
                    rc_s.at[spot],
                    rc_r.at[spot],
                    flip_rp(dx, dc),
                    flip_re(dl),
                )
                c_copies.append((spot, copy))
    summed = rates_b[x_lo]
    for spot, copy in reversed(c_copies):
        copy.wait_recv()
        summed = summed + land_c[spot]
    rates_z[...] = summed
    z_copies = []
    for step in (4, 3, 5, 2, 6, 1, 7):
        copy = remote(
            rates_z, land_z.at[step], rz_s.at[step], rz_r.at[step], along_z(step), re
        )
        z_copies.append((step, copy))
    for step, copy in reversed(z_copies):
        copy.wait_recv()
        summed = summed + land_z[step]
    out_ref[0:8, :] = summed[:, 0:40]
    out_ref[8:16, :] = summed[:, 40:80]

    for copy in started:
        copy.wait_send()


def per_device(
    wannier_coupling,
    phonon_lattice,
    phonon_degeneracy,
    electron_lattice,
    electron_degeneracy,
    phonon_wavevectors,
    electron_wavevectors,
    phonon_energies,
    bloch_rotations,
    band_energies,
    shifted_points,
):
    def vm(shape, dtype):
        return pltpu.VMEM(shape, dtype)

    def dma(*shape):
        return pltpu.SemaphoreType.DMA(shape)

    return pl.pallas_call(
        kernel,
        out_shape=jax.ShapeDtypeStruct((16, 40), F32),
        in_specs=[pl.BlockSpec(memory_space=pltpu.VMEM)] * 11,
        out_specs=pl.BlockSpec(memory_space=pltpu.VMEM),
        scratch_shapes=[
            vm((64, LANES), BF),
            vm((64, LANES), BF),
            vm((32, 128), BF),
            vm((32, 128), BF),
            vm((256, 128), BF),
            vm((256, 128), BF),
            vm((256, 128), BF),
            vm((16, 16), jnp.int32),
            vm((4, 128, 128), F32),
            vm((144, PACK), BF),
            vm((2, 144, PACK), BF),
            vm((8, 2, 16, PACK), BF),
            vm((16, 2, 16, PACK), BF),
            vm((256, LANES), F32),
            vm((2, 2, 16, LANES), BF),
            vm((2, 2, 16, LANES), BF),
            vm((2, 16, LANES), BF),
            vm((2, 16, LANES), BF),
            vm((2, 2, 16, LANES), BF),
            vm((2, 2, 16, LANES), BF),
            vm((2, 2, 16, LANES), BF),
            vm((2, 2, 16, LANES), BF),
            vm((2, 2, 8, LANES), F32),
            vm((4, 8, LANES), F32),
            vm((8, 16, LANES), BF),
            vm((64, 128), BF),
            vm((2560, 128), F32),
            vm((2560, 128), F32),
            vm((32, 80, 256), BF),
            vm((32, 48, 128), BF),
            vm((1280, 128), F32),
            vm((32, 128), F32),
            vm((1280, 128), F32),
            vm((1280, 128), F32),
            vm((32, 128), F32),
            vm((2, 8, 128), F32),
            vm((8, 8, 128), F32),
            vm((8, 128), F32),
            vm((8, 8, 128), F32),
            dma(2),
            dma(2),
            pltpu.SemaphoreType.DMA,
            pltpu.SemaphoreType.DMA,
            dma(16),
            dma(16),
            dma(2, 2),
            dma(2, 2),
            dma(2),
            dma(2),
            dma(2),
            dma(2),
            dma(2, 2),
            dma(2, 2),
            dma(4),
            dma(4),
            dma(5),
            dma(5),
            dma(4),
            dma(4),
            dma(8),
            dma(8),
            dma(8),
            dma(8),
        ],
        compiler_params=pltpu.CompilerParams(
            collective_id=0, has_side_effects=True, vmem_limit_bytes=40 * 1024 * 1024
        ),
        cost_estimate=pl.CostEstimate(
            flops=300_000_000, bytes_accessed=2_000_000, transcendentals=200_000
        ),
    )(
        wannier_coupling,
        phonon_lattice,
        phonon_degeneracy.reshape(4, 1),
        electron_lattice.T,
        electron_degeneracy.reshape(1, 64),
        phonon_wavevectors.T,
        electron_wavevectors.T,
        phonon_energies,
        bloch_rotations,
        band_energies,
        shifted_points,
    )


def solution(mesh):
    in_specs = (
        P("re", "rp", None),
        P("rp", None),
        P("rp"),
        P(),
        P(),
        P(),
        P("re", None),
        P("rp", None),
        P("re", None),
        P("re", None),
        P("rp", None),
    )
    return jax.shard_map(
        per_device, mesh=mesh, in_specs=in_specs, out_specs=P("re", None), check_vma=False
    )
```

time: 85.5 us -> 64.5 us (0.75)
  Pallas kernels: 77.3 us -> 57.6 us
  other arithmetic: 2.1 us -> 0 us
  local copies, waits for them, and re-layouts: 4.42 us -> 5.95 us
  matrix products: 1.3 us -> 0 us
    pallas_call x1, Pallas kernels: 77.3 us -> 57.6 us  [per_device(): pl.pallas_call(kernel, out_shape=jax.ShapeDtypeStruct((16, 40), F32), in_...]
    unnamed x16 -> x21, local copies, waits for them, and re-layouts: 3.15 us -> 5.17 us
    dot_general x2 -> x0, matrix products: 1.3 us -> none  [phase_tables(): jnp.dot(points, lattice.astype(F32).T, precision=highest)]
where the time goes in v2:
time: 64.5 us; the launch traced here: 63.6 us
  Pallas kernels  57.6 us (89%)
  local copies, waits for them, and re-layouts  5.95 us (9%)
    pallas_call x1, Pallas kernels, per_device(): pl.pallas_call(kernel, out_shape=jax.ShapeDtypeStruct((16, 40), F32), in_...  57.6 us
    unnamed x21, local copies, waits for them, and re-layouts  5.17 us

profile of v2, /device:TPU:1, one launch (start us, length us, event | category | flops | bytes accessed | tf_op | source)
XLA Modules:
  0.0 63.6 jit_solution(15438677194677838925)
XLA Ops:
  0.0 0.0 copy-start.2
  0.0 0.0 copy-start.3
  0.0 0.0 copy-start.7
  0.0 0.0 copy-start.8
  0.0 0.8 %copy.12.pdeg_ref = s32[4,1]{1,0:T(4,128)S(1)} copy(s32[4,1]{0,1:T(1,128)} %bitcast.9) | data formatting | bytes 32 | tf_op jit(solution)/shard_map/reshape | solution.py:660
  0.8 0.0 copy-done.2
  0.8 0.0 copy-done.3
  0.8 0.0 copy-done.7
  0.8 0.0 copy-done.8
  0.8 0.0 copy-start
  0.8 0.9 %copy-done = bf16[4,4,6400]{2,1,0:T(4,128)(2,1)S(1)} copy-done((bf16[4,4,6400]{2,1,0:T(4,128)(2,1)S(1)}, bf16[4,4,6400]{2,1,0:T(4,128)(2,1)}, u32[]{:S(2)}) %copy-start) | copy-done | bytes 204824
  1.8 0.0 copy-start.1
  1.8 0.9 %copy-done.1 = f32[16,3200]{1,0:T(8,128)S(1)} copy-done((f32[16,3200]{1,0:T(8,128)S(1)}, f32[16,3200]{1,0:T(8,128)}, u32[]{:S(2)}) %copy-start.1) | copy-done | bytes 204824
  2.7 0.0 copy-start.4
  2.7 0.7 %copy-done.4 = s32[64,3]{0,1:T(4,128)S(1)} copy-done((s32[64,3]{0,1:T(4,128)S(1)}, s32[64,3]{0,1:T(4,128)}, u32[]{:S(2)}) %copy-start.4) | copy-done | bytes 792
  3.4 0.0 copy-start.5
  3.4 0.7 %copy-done.5 = f32[32,3]{0,1:T(4,128)S(1)} copy-done((f32[32,3]{0,1:T(4,128)S(1)}, f32[32,3]{0,1:T(4,128)}, u32[]{:S(2)}) %copy-start.5) | copy-done | bytes 408
  4.0 0.0 copy-start.6
  4.1 0.7 %copy-done.6 = f32[16,3]{0,1:T(4,128)S(1)} copy-done((f32[16,3]{0,1:T(4,128)S(1)}, f32[16,3]{0,1:T(4,128)}, u32[]{:S(2)}) %copy-start.6) | copy-done | bytes 216
  4.7 0.0 copy-start.9
  4.7 0.7 %copy-done.9 = f32[1,2]{1,0:T(1,128)S(1)} copy-done((f32[1,2]{1,0:T(1,128)S(1)}, f32[1,2]{1,0:T(1,128)}, u32[]{:S(2)}) %copy-start.9) | copy-done | bytes 32
  5.4 57.6 %shard_map.109 = f32[16,40]{1,0:T(8,128)S(1)} custom-call(bf16[4,4,6400]{2,1,0:T(4,128)(2,1)S(1)} %copy-done, s32[4,3]{1,0:T(4,128)S(1)} %copy-done.3, s32[4,1]{1,0:T(4,128)S(1)} %copy.12.pdeg_ref, s32[3,64]{1,0:T(4,128)S(1)} %bitcast.5, s32[1,64]{1,0:T(1,128)S(1)} %bitcast.8, f32[3,32]{1,0:T(4,128)S(1)} %bitcast.6, f32[3,16]{1,0:T(4,128)S(1)} %bitcast.7, ...), custom_call_target="tpu_custom_call" | custom-call | flops 300000000 | bytes 2000000 | tf_op jit(solution)/shard_map/pallas_call | solution.py:581
  63.0 0.6 copy.14
Async XLA Ops:
  0.0 0.8 %copy-start.2 = (f32[16,40]{1,0:T(8,128)S(1)}, f32[16,40]{1,0:T(8,128)}, u32[]{:S(2)}) copy-start(f32[16,40]{1,0:T(8,128)} %band_ref.1) | copy-start | bytes 7684
  0.0 0.8 %copy-start.3 = (s32[4,3]{1,0:T(4,128)S(1)}, s32[4,3]{1,0:T(4,128)}, u32[]{:S(2)}) copy-start(s32[4,3]{1,0:T(4,128)} %plat_ref.1) | copy-start | bytes 148
  0.0 0.8 %copy-start.7 = (s32[1,256]{1,0:T(1,128)S(1)}, s32[1,256]{1,0:T(1,128)}, u32[]{:S(2)}) copy-start(s32[1,256]{1,0:T(1,128)} %shift_ref.1) | copy-start | bytes 3076
  0.0 0.8 %copy-start.8 = (s32[64]{0:T(128)S(1)}, s32[64]{0:T(128)}, u32[]{:S(2)}) copy-start(s32[64]{0:T(128)} %param.15) | copy-start | bytes 772
  0.8 0.9 %copy-start = (bf16[4,4,6400]{2,1,0:T(4,128)(2,1)S(1)}, bf16[4,4,6400]{2,1,0:T(4,128)(2,1)}, u32[]{:S(2)}) copy-start(bf16[4,4,6400]{2,1,0:T(4,128)(2,1)} %w_ref.1) | copy-start | bytes 614404
  1.8 0.9 %copy-start.1 = (f32[16,3200]{1,0:T(8,128)S(1)}, f32[16,3200]{1,0:T(8,128)}, u32[]{:S(2)}) copy-start(f32[16,3200]{1,0:T(8,128)} %rot_ref.1) | copy-start | bytes 614404
  2.7 0.7 %copy-start.4 = (s32[64,3]{0,1:T(4,128)S(1)}, s32[64,3]{0,1:T(4,128)}, u32[]{:S(2)}) copy-start(s32[64,3]{0,1:T(4,128)} %param.14) | copy-start | bytes 2308
  3.4 0.7 %copy-start.5 = (f32[32,3]{0,1:T(4,128)S(1)}, f32[32,3]{0,1:T(4,128)}, u32[]{:S(2)}) copy-start(f32[32,3]{0,1:T(4,128)} %param.16) | copy-start | bytes 1156
  4.0 0.7 %copy-start.6 = (f32[16,3]{0,1:T(4,128)S(1)}, f32[16,3]{0,1:T(4,128)}, u32[]{:S(2)}) copy-start(f32[16,3]{0,1:T(4,128)} %param.17) | copy-start | bytes 580
  4.7 0.7 %copy-start.9 = (f32[1,2]{1,0:T(1,128)S(1)}, f32[1,2]{1,0:T(1,128)}, u32[]{:S(2)}) copy-start(f32[1,2]{1,0:T(1,128)} %phonon_ref.1) | copy-start | bytes 28

commit v3 on v2

--- a/solution.py
+++ b/solution.py
@@ -48,6 +48,18 @@
 
 
 def kernel(
+    w_hbm,
+    plat_hbm,
+    pdeg_hbm,
+    elat_hbm,
+    edeg_hbm,
+    qvec_hbm,
+    kvec_hbm,
+    phonon_hbm,
+    rot_hbm,
+    band_hbm,
+    shift_hbm,
+    out_ref,
     w_ref,
     plat_ref,
     pdeg_ref,
@@ -59,7 +71,6 @@
     rot_ref,
     band_ref,
     shift_ref,
-    out_ref,
     w_own,
     w_sib,
     cosw,
@@ -78,12 +89,8 @@
     l_far,
     s_opp,
     l_opp,
-    s_near,
-    l_near,
-    s_two,
-    l_two,
-    total,
-    land_x,
+    s_piece,
+    l_piece,
     waves,
     mix,
     turn_a,
@@ -99,6 +106,7 @@
     land_c,
     rates_z,
     land_z,
+    in_s,
     core_s,
     core_r,
     pack_s,
@@ -109,12 +117,10 @@
     far_r,
     opp_s,
     opp_r,
-    near_s,
-    near_r,
-    two_s,
-    two_r,
-    x_s,
-    x_r,
+    piece_s,
+    piece_r,
+    swap_s,
+    swap_r,
     y1_s,
     y1_r,
     y2_s,
@@ -132,10 +138,10 @@
     y = re // 2
     x_lo = re % 2
 
-    def flip_rp(dx, dc):
+    def flip_rp(dx, dc, step=0):
         hi = (1 - x_hi) if dx else x_hi
         co = (1 - core) if dc else core
-        return z * 4 + hi * 2 + co
+        return ((z + 8 + step) % 8) * 4 + hi * 2 + co
 
     def flip_re(dl):
         return y * 2 + ((1 - x_lo) if dl else x_lo)
@@ -145,6 +151,29 @@
 
     def along_y(step):
         return (re + 16 + 2 * step) % 16
+
+    loads = {}
+    for number, (name, src, dst) in enumerate(
+        (
+            ("w", w_hbm, w_ref),
+            ("plat", plat_hbm, plat_ref),
+            ("pdeg", pdeg_hbm, pdeg_ref),
+            ("qvec", qvec_hbm, qvec_ref),
+            ("elat", elat_hbm, elat_ref),
+            ("edeg", edeg_hbm, edeg_ref),
+            ("kvec", kvec_hbm, kvec_ref),
+            ("phonon", phonon_hbm, phonon_ref),
+            ("rot", rot_hbm, rot_ref),
+            ("band", band_hbm, band_ref),
+            ("shift", shift_hbm, shift_ref),
+        )
+    ):
+        loads[name] = pltpu.make_async_copy(src, dst, in_s.at[number])
+        loads[name].start()
+
+    def loaded(*names):
+        for name in names:
+            loads[name].wait()
 
     started = []
 
@@ -161,30 +190,44 @@
         started.append(copy)
         return copy
 
-    partners = [(rp, (re + step) % 16) for step in range(1, 16)]
+    partners = [
+        (flip_rp(dx, dc), flip_re(dl))
+        for dc in (1, 0)
+        for dx in (0, 1)
+        for dl in (0, 1)
+        if dx or dc or dl
+    ]
     partners += [(along_z(step), re) for step in range(1, 8)]
     partners += [
-        (flip_rp(dx, dc), flip_re(dl))
-        for dx in (0, 1)
-        for dc in (0, 1)
-        for dl in (0, 1)
-        if dx or dc
+        (flip_rp(dx, 0, step), flip_re(dl))
+        for step in (1, -1, 2, -2)
+        for dx, dl in ((0, 1), (1, 0), (1, 1))
     ]
+    partners += [(rp, along_y(step)) for step in range(1, 8)]
     barrier = pltpu.get_barrier_semaphore()
     for to_rp, to_re in partners:
         pl.semaphore_signal(
             barrier, inc=1, device_id={"rp": to_rp, "re": to_re}, device_id_type=MESH
         )
 
+    loaded("w")
     cells = jnp.concatenate([w_ref[e].astype(F32) for e in range(4)], axis=0)
     for mc in range(4):
         w_own[mc * 16 : mc * 16 + 16, :] = jnp.concatenate(
             [cells[:, mc * ROW : (mc + 1) * ROW], jnp.zeros((16, LANES - ROW), F32)], axis=1
         ).astype(BF)
 
+    pl.semaphore_wait(barrier, len(partners))
+
+    sib = flip_rp(0, 1)
+    core_copies = [remote(w_own, w_sib, core_s.at[0], core_r.at[0], sib, re)]
+
+    loaded("plat", "pdeg", "qvec")
     r_of_lane = jnp.where(iota((4, 128), 0) == (iota((4, 128), 1) & 3), 1.0, 0.0).astype(F32)
     p_angle = full_turn * outer(qvec_ref[...], outer(plat_ref[...].astype(F32), r_of_lane))
-    p_weight = 1.0 / outer(pdeg_ref[...].astype(F32), r_of_lane)
+    p_weight = 1.0 / jnp.dot(
+        pdeg_ref[...].astype(F32), r_of_lane, precision=highest, preferred_element_type=F32
+    )
     cosw[...] = (jnp.cos(p_angle) * p_weight).astype(BF)
     sinw[...] = (jnp.sin(p_angle) * p_weight).astype(BF)
     row = iota((256, 128), 0)
@@ -208,14 +251,7 @@
 
     lhs_out[...] = phases_for(1 - core)
 
-    pl.semaphore_wait(barrier, len(partners))
-
-    sib = flip_rp(0, 1)
-    core_copies = [
-        remote(w_own, w_sib, core_s.at[0], core_r.at[0], sib, re),
-        remote(lhs_out, lhs_sib, core_s.at[1], core_r.at[1], sib, re),
-    ]
-
+    core_copies.append(remote(lhs_out, lhs_sib, core_s.at[1], core_r.at[1], sib, re))
     lhs_own[...] = phases_for(core)
     for start, end in LANE_TILES:
         part[:, start:end] = mm(lhs_own[:, 0:64], w_own[:, start:end])
@@ -247,14 +283,35 @@
                 along_z(step),
                 re,
             )
-    near = {}
-    for side, step in ((0, 1), (1, -1)):
-        for sub in (0, 1):
-            s_near[side, sub] = part_of(z + step, sub).astype(BF)
-        near[side] = remote(
-            s_near.at[side], l_near.at[side], near_s.at[side], near_r.at[side], along_z(step), re
-        )
-
+
+    def piece_of(z_to, dx, dl):
+        hi = (1 - x_hi) if dx else x_hi
+        mode = (x_lo + dl) % 2
+        first_row = (((z_to + 8) % 8) * 2 + hi) * 16 + mode * 8
+        rows = part[pl.ds(pl.multiple_of(first_row, 8), 8), :]
+        end = jnp.concatenate([rows[:, HALF:], jnp.zeros((8, 2 * HALF - LANES), F32)], axis=1)
+        return jnp.concatenate([rows[:, 0:HALF], end], axis=0).astype(BF)
+
+    pieces = {}
+
+    def send_piece(place, step, dx, dl):
+        s_piece[dl, dx, place] = piece_of(z + step, dx, dl)
+        pieces[dl, dx, place] = remote(
+            s_piece.at[dl, dx, place],
+            l_piece.at[dl, dx, place],
+            piece_s.at[dl, dx, place],
+            piece_r.at[dl, dx, place],
+            flip_rp(dx, 0, step),
+            flip_re(dl),
+        )
+
+    for dx, dl in ((1, 1), (1, 0), (0, 1), (0, 0)):
+        for place, step in ((1, 1), (2, -1)):
+            send_piece(place, step, dx, dl)
+    for dx, dl in ((1, 1), (1, 0), (0, 1)):
+        send_piece(0, 0, dx, dl)
+
+    loaded("elat", "edeg", "kvec", "phonon", "rot", "band", "shift")
     e_angle = full_turn * outer(kvec_ref[...], elat_ref[...].astype(F32))
     e_weight = 1.0 / edeg_ref[...].astype(F32)
     high, middle, low = three_parts(band_ref[...])
@@ -293,31 +350,32 @@
     take = jnp.where(take, 1.0, 0.0).astype(BF)
     u_out[...] = mm(take, pack[0:128, :]).astype(BF).reshape(8, 2, 16, PACK)
     u_copies = []
-    for step in range(1, 16):
-        to = (re + step) % 16
+    for step in (4, 3, 5, 2, 6, 1, 7):
         u_copies.append(
-            remote(u_out.at[to // 2], u_in.at[re], u_s.at[step], u_r.at[step], rp, to)
+            remote(
+                u_out.at[(y + step) % 8],
+                u_in.at[x_lo, y],
+                u_s.at[step],
+                u_r.at[step],
+                rp,
+                along_y(step),
+            )
         )
     packs[x_lo] = pack[...]
-    u_in[re] = u_out[y]
-
-    two = {}
+    u_in[x_lo, y] = u_out[y]
+
     for sub in (0, 1):
         for side, step in ((0, 1), (1, -1)):
             far[side, sub].wait_recv()
-            done = part_of(z + 2 * step, sub) + l_far[side, sub].astype(F32)
+            more = l_far[side, sub].astype(F32)
             if side == sub:
                 opp[sub].wait_recv()
-                done = done + l_opp[sub].astype(F32)
-            s_two[side, sub] = done.astype(BF)
-            two[side, sub] = remote(
-                s_two.at[side, sub],
-                l_two.at[side, sub],
-                two_s.at[side, sub],
-                two_r.at[side, sub],
-                along_z(2 * step),
-                re,
-            )
+                more = more + l_opp[sub].astype(F32)
+            hi = (1 - x_hi) if sub == 0 else x_hi
+            block = ((z + 8 + 2 * step) % 8) * 2 + hi
+            part[pl.ds(pl.multiple_of(block * 16, 16), 16), :] += more
+            for dl in (1, 0):
+                send_piece(3 + side, 2 * step, 1 - sub, dl)
 
     def swap_halves(rows):
         cut = rows.reshape(16, 8, PACK)
@@ -348,8 +406,7 @@
         lax.fori_loop(0, 32, one, 0)
 
     def rotations_there():
-        for copy in u_copies:
-            copy.wait_recv()
+        u_swap.wait_recv()
         blank = jnp.zeros((128, 88), F32)
         for b in (0, 1):
             block = points_ref[pl.ds(y * 2 + b, 1), :]
@@ -358,9 +415,10 @@
             target = jnp.sum(jnp.where(spot, wide, 0), axis=1, keepdims=True)
             before = ((wide >> 4) == (target >> 4)) & (wide < target)
             second = jnp.max(jnp.where(before, 1, 0), axis=1, keepdims=True)
-            source = (target >> 4) * 16 + second * 8 + (iota((128, 1), 0) & 7)
+            source = ((target >> 4) & 1) * 128 + (target >> 5) * 16 + second * 8
+            source = source + (iota((128, 1), 0) & 7)
             order = jnp.where(iota((128, 256), 1) == source, 1.0, 0.0).astype(BF)
-            rows = mm(order, u_in[:, b].reshape(256, PACK))
+            rows = mm(order, u_in[:, :, b].reshape(256, PACK))
             for t in range(10):
                 turn_a[pl.ds(b * 1280 + t, 128, stride=10), :] = jnp.concatenate(
                     [rows[:, t * 40 : t * 40 + 40], blank], axis=1
@@ -423,41 +481,32 @@
     rotations_here()
     electron_phases()
 
-    x_copies = {}
-    for side in (0, 1):
-        near[side].wait_recv()
-    for sub in (0, 1):
-        done = part_of(z, sub) + l_near[0, sub].astype(F32) + l_near[1, sub].astype(F32)
-        for side in (0, 1):
-            two[side, sub].wait_recv()
-            done = done + l_two[side, sub].astype(F32)
-        total[sub] = done.reshape(2, 8, LANES)
-        for dl in (0, 1):
-            if sub == 1 and dl == 0:
-                continue
-            dx = 1 - sub
-            spot = dx * 2 + dl
-            x_copies[spot] = remote(
-                total.at[sub, (x_lo + dl) % 2],
-                land_x.at[spot],
-                x_s.at[spot],
-                x_r.at[spot],
-                flip_rp(dx, 0),
-                flip_re(dl),
-            )
-    rotations_there()
-    for copy in x_copies.values():
+    for copy in u_copies:
         copy.wait_recv()
-    waves[0] = jnp.concatenate(
-        [total[1, x_lo] + land_x[2], land_x[1] + land_x[3]], axis=0
-    ).astype(BF)
+    u_swap = remote(u_in.at[x_lo], u_in.at[x_lo], swap_s, swap_r, rp, flip_re(1))
+    for copy in pieces.values():
+        copy.wait_recv()
+    own_row = (z * 2 + x_hi) * 16 + x_lo * 8
+    blocks = []
+    for dl in (0, 1):
+        added = None
+        for dx in (0, 1):
+            for place in range(5):
+                if dl == 0 and dx == 0 and place == 0:
+                    continue
+                piece = l_piece[dl, dx, place].astype(F32)
+                added = piece if added is None else added + piece
+        block = jnp.concatenate([added[0:8], added[8:16, 0 : LANES - HALF]], axis=1)
+        if dl == 0:
+            block = block + part[pl.ds(pl.multiple_of(own_row, 8), 8), :]
+        blocks.append(block)
+    waves[0] = jnp.concatenate(blocks, axis=0).astype(BF)
 
     first = {}
-    for place, step in ((4, 2), (3, -2), (2, 1), (1, -1)):
+    for place, step in ((2, 1), (1, -1), (4, 2), (3, -2)):
         first[place] = remote(
             waves.at[0], waves.at[place], y1_s.at[place], y1_r.at[place], rp, along_y(step)
         )
-    weights()
     first[2].wait_recv()
     later = [remote(waves.at[2], waves.at[6], y2_s.at[0], y2_r.at[0], rp, along_y(2))]
     first[1].wait_recv()
@@ -486,6 +535,8 @@
             along_y(-2),
         )
     )
+    rotations_there()
+    weights()
     points_c = mm(mix[:, 0:80], waves[0:5].reshape(80, LANES))
     for copy in later:
         copy.wait_recv()
@@ -581,9 +632,20 @@
     return pl.pallas_call(
         kernel,
         out_shape=jax.ShapeDtypeStruct((16, 40), F32),
-        in_specs=[pl.BlockSpec(memory_space=pltpu.VMEM)] * 11,
+        in_specs=[pl.BlockSpec(memory_space=pl.ANY)] * 11,
         out_specs=pl.BlockSpec(memory_space=pltpu.VMEM),
         scratch_shapes=[
+            vm((4, 4, 6400), BF),
+            vm((4, 3), jnp.int32),
+            vm((1, 4), jnp.int32),
+            vm((3, 64), jnp.int32),
+            vm((1, 64), jnp.int32),
+            vm((3, 32), F32),
+            vm((3, 16), F32),
+            vm((1, 2), F32),
+            vm((16, 3200), F32),
+            vm((16, 40), F32),
+            vm((1, 256), jnp.int32),
             vm((64, LANES), BF),
             vm((64, LANES), BF),
             vm((32, 128), BF),
@@ -596,18 +658,14 @@
             vm((144, PACK), BF),
             vm((2, 144, PACK), BF),
             vm((8, 2, 16, PACK), BF),
-            vm((16, 2, 16, PACK), BF),
+            vm((2, 8, 2, 16, PACK), BF),
             vm((256, LANES), F32),
             vm((2, 2, 16, LANES), BF),
             vm((2, 2, 16, LANES), BF),
             vm((2, 16, LANES), BF),
             vm((2, 16, LANES), BF),
-            vm((2, 2, 16, LANES), BF),
-            vm((2, 2, 16, LANES), BF),
-            vm((2, 2, 16, LANES), BF),
-            vm((2, 2, 16, LANES), BF),
-            vm((2, 2, 8, LANES), F32),
-            vm((4, 8, LANES), F32),
+            vm((2, 2, 5, 16, HALF), BF),
+            vm((2, 2, 5, 16, HALF), BF),
             vm((8, 16, LANES), BF),
             vm((64, 128), BF),
             vm((2560, 128), F32),
@@ -623,22 +681,21 @@
             vm((8, 8, 128), F32),
             vm((8, 128), F32),
             vm((8, 8, 128), F32),
+            dma(11),
             dma(2),
             dma(2),
             pltpu.SemaphoreType.DMA,
             pltpu.SemaphoreType.DMA,
-            dma(16),
-            dma(16),
+            dma(8),
+            dma(8),
             dma(2, 2),
             dma(2, 2),
             dma(2),
             dma(2),
-            dma(2),
-            dma(2),
-            dma(2, 2),
-            dma(2, 2),
-            dma(4),
-            dma(4),
+            dma(2, 2, 5),
+            dma(2, 2, 5),
+            pltpu.SemaphoreType.DMA,
+            pltpu.SemaphoreType.DMA,
             dma(5),
             dma(5),
             dma(4),
@@ -649,7 +706,7 @@
             dma(8),
         ],
         compiler_params=pltpu.CompilerParams(
-            collective_id=0, has_side_effects=True, vmem_limit_bytes=40 * 1024 * 1024
+            collective_id=0, has_side_effects=True, vmem_limit_bytes=60 * 1024 * 1024
         ),
         cost_estimate=pl.CostEstimate(
             flops=300_000_000, bytes_accessed=2_000_000, transcendentals=200_000
@@ -657,7 +714,7 @@
     )(
         wannier_coupling,
         phonon_lattice,
-        phonon_degeneracy.reshape(4, 1),
+        phonon_degeneracy.reshape(1, 4),
         electron_lattice.T,
         electron_degeneracy.reshape(1, 64),
         phonon_wavevectors.T,

time: 64.5 us -> 59.2 us (0.918)
  local copies, waits for them, and re-layouts: 5.95 us -> 1.3 us
    unnamed x21 -> x1, local copies, waits for them, and re-layouts: 5.17 us -> 1.3 us
    reshape x1 -> x0, local copies, waits for them, and re-layouts: 0.78 us -> none  [per_device(): phonon_degeneracy.reshape(4, 1)]
where the time goes in v3:
time: 59.2 us; the launch traced here: 58.3 us
  Pallas kernels  57 us (96%)
  local copies, waits for them, and re-layouts  1.3 us (2%)
    pallas_call x1, Pallas kernels, per_device(): pl.pallas_call(kernel, out_shape=jax.ShapeDtypeStruct((16, 40), F32), in_...  57 us
    unnamed x1, local copies, waits for them, and re-layouts  1.3 us

profile of v3, /device:TPU:1, one launch (start us, length us, event | category | flops | bytes accessed | tf_op | source)
XLA Modules:
  0.0 58.3 jit_solution(6294155137994449382)
XLA Ops:
  0.0 57.0 %shard_map.109 = f32[16,40]{1,0:T(8,128)} custom-call(bf16[4,4,6400]{2,1,0:T(4,128)(2,1)} %w_hbm.1, s32[4,3]{1,0:T(4,128)} %plat_hbm.1, s32[1,4]{1,0:T(1,128)} %bitcast.8, s32[3,64]{1,0:T(4,128)} %bitcast.5, s32[1,64]{1,0:T(1,128)} %bitcast.9, f32[3,32]{1,0:T(4,128)} %bitcast.6, f32[3,16]{1,0:T(4,128)} %bitcast.7, f32[1,2]{1,0:T(1,128)} %phonon_hbm.1, ...), custom_call_target="tpu_custom_call" | custom-call | flops 300000000 | bytes 2000000 | tf_op jit(solution)/shard_map/pallas_call | solution.py:632
  57.0 1.3 %copy.13 = f32[16,40]{1,0:T(8,128)} copy(f32[16,40]{1,0:T(8,128)} %shard_map.109) | data formatting | bytes 5120

commit v4 on v3

--- a/solution.py
+++ b/solution.py
@@ -99,6 +99,7 @@
     left_rot,
     energy_col,
     energy_row,
+    length_row,
     weight,
     coupling,
     rates,
@@ -153,9 +154,55 @@
         return (re + 16 + 2 * step) % 16
 
     loads = {}
+
+    def load(name, src, dst, number):
+        loads[name] = pltpu.make_async_copy(src, dst, in_s.at[number])
+        loads[name].start()
+
+    for e in range(4):
+        load(f"w{e}", w_hbm.at[e], w_ref.at[e], e)
+
+    def loaded(*names):
+        for name in names:
+            loads[name].wait()
+
+    started = []
+
+    def remote(src, dst, send, recv, to_rp, to_re):
+        copy = pltpu.make_async_remote_copy(
+            src_ref=src,
+            dst_ref=dst,
+            send_sem=send,
+            recv_sem=recv,
+            device_id={"rp": to_rp, "re": to_re},
+            device_id_type=MESH,
+        )
+        copy.start()
+        started.append(copy)
+        return copy
+
+    partners = []
+    for step in (4, 3, -3, 2, -2, 1, -1):
+        partners += [(rp, along_y(step)), (along_z(step), re)]
+        if abs(step) < 3:
+            partners += [
+                (flip_rp(dx, 0, step), flip_re(dl)) for dx, dl in ((1, 1), (1, 0), (0, 1))
+            ]
+    partners += [
+        (flip_rp(dx, dc), flip_re(dl))
+        for dc in (0, 1)
+        for dx in (1, 0)
+        for dl in (1, 0)
+        if dx or dc or dl
+    ]
+    barrier = pltpu.get_barrier_semaphore()
+    for to_rp, to_re in partners:
+        pl.semaphore_signal(
+            barrier, inc=1, device_id={"rp": to_rp, "re": to_re}, device_id_type=MESH
+        )
+
     for number, (name, src, dst) in enumerate(
         (
-            ("w", w_hbm, w_ref),
             ("plat", plat_hbm, plat_ref),
             ("pdeg", pdeg_hbm, pdeg_ref),
             ("qvec", qvec_hbm, qvec_ref),
@@ -168,49 +215,9 @@
             ("shift", shift_hbm, shift_ref),
         )
     ):
-        loads[name] = pltpu.make_async_copy(src, dst, in_s.at[number])
-        loads[name].start()
-
-    def loaded(*names):
-        for name in names:
-            loads[name].wait()
-
-    started = []
-
-    def remote(src, dst, send, recv, to_rp, to_re):
-        copy = pltpu.make_async_remote_copy(
-            src_ref=src,
-            dst_ref=dst,
-            send_sem=send,
-            recv_sem=recv,
-            device_id={"rp": to_rp, "re": to_re},
-            device_id_type=MESH,
-        )
-        copy.start()
-        started.append(copy)
-        return copy
-
-    partners = [
-        (flip_rp(dx, dc), flip_re(dl))
-        for dc in (1, 0)
-        for dx in (0, 1)
-        for dl in (0, 1)
-        if dx or dc or dl
-    ]
-    partners += [(along_z(step), re) for step in range(1, 8)]
-    partners += [
-        (flip_rp(dx, 0, step), flip_re(dl))
-        for step in (1, -1, 2, -2)
-        for dx, dl in ((0, 1), (1, 0), (1, 1))
-    ]
-    partners += [(rp, along_y(step)) for step in range(1, 8)]
-    barrier = pltpu.get_barrier_semaphore()
-    for to_rp, to_re in partners:
-        pl.semaphore_signal(
-            barrier, inc=1, device_id={"rp": to_rp, "re": to_re}, device_id_type=MESH
-        )
-
-    loaded("w")
+        load(name, src, dst, 4 + number)
+
+    loaded("w0", "w1", "w2", "w3")
     cells = jnp.concatenate([w_ref[e].astype(F32) for e in range(4)], axis=0)
     for mc in range(4):
         w_own[mc * 16 : mc * 16 + 16, :] = jnp.concatenate(
@@ -315,12 +322,6 @@
     e_angle = full_turn * outer(kvec_ref[...], elat_ref[...].astype(F32))
     e_weight = 1.0 / edeg_ref[...].astype(F32)
     high, middle, low = three_parts(band_ref[...])
-    gap = jnp.zeros((16, 48), F32)
-    pack[128:144, :] = jnp.concatenate(
-        [jnp.cos(e_angle) * e_weight, jnp.sin(e_angle) * e_weight]
-        + [high, high, gap, middle, middle, gap, low, low, gap],
-        axis=1,
-    ).astype(BF)
     rest = jnp.zeros((16, PACK - 415), F32)
     for j in range(8):
         five = slice(j * 5, j * 5 + 5)
@@ -332,6 +333,20 @@
             pack_f[v, pl.ds(j, 16, stride=8), :] = eighth[:, v * 128 : v * 128 + 128]
     for v in range(4):
         pack[0:128, v * 128 : v * 128 + 128] = pack_f[v].astype(BF)
+    exact = jnp.concatenate([pack_f[v] for v in range(4)], axis=1)
+    kept = pack[0:128, :].astype(F32)
+    took = (exact - kept) * (exact + kept)
+    left = kept * kept
+    took = sum(took[:, t * 40 : t * 40 + 40] for t in range(10)).reshape(16, 8, 40)
+    left = sum(left[:, t * 40 : t * 40 + 40] for t in range(10)).reshape(16, 8, 40)
+    took, left = jnp.sum(took, axis=1), jnp.sum(left, axis=1)
+    short = jnp.where(left > 0.0, took / jnp.where(left > 0.0, left, 1.0), 0.0)
+    gap = jnp.zeros((16, 48), F32)
+    pack[128:144, :] = jnp.concatenate(
+        [jnp.cos(e_angle) * e_weight, jnp.sin(e_angle) * e_weight]
+        + [high, high, short, gap[:, 0:8], middle, middle, gap, low, low, gap],
+        axis=1,
+    ).astype(BF)
     pack_copy = remote(pack, packs.at[x_lo], pack_s, pack_r, rp, flip_re(1))
 
     for d in range(16):
@@ -397,13 +412,19 @@
             energy_row[b * 16 : b * 16 + 16, :] = (
                 tail[:, 128:256] + tail[:, 256:384] + tail[:, 384:512]
             )
-
-        def one(i, carry):
-            spot = pl.ds(pl.multiple_of(i * 80, 8), 80)
-            right_rot[i] = jnp.concatenate([turn_a[spot, :], turn_b[spot, :]], axis=1).astype(BF)
+            gain = 1.0 + tail[:, 208:248]
+            length_row[b * 16 : b * 16 + 16, :] = jnp.concatenate(
+                [gain, gain, jnp.zeros((16, 48), F32)], axis=1
+            )
+
+        def some(group, carry):
+            for i in [group * 8 + member for member in range(8)]:
+                spot = pl.ds(pl.multiple_of(i * 80, 8), 80)
+                both = [turn_a[spot, :], turn_b[spot, :]]
+                right_rot[i] = jnp.concatenate(both, axis=1).astype(BF)
             return carry
 
-        lax.fori_loop(0, 32, one, 0)
+        lax.fori_loop(0, 4, some, 0)
 
     def rotations_there():
         u_swap.wait_recv()
@@ -433,33 +454,46 @@
                     energy, (128, 128)
                 )
 
-        def one(i, carry):
-            spot = pl.ds(pl.multiple_of(i * 80, 8), 80)
-            left_rot[i, :, 0:80] = jnp.transpose(turn_a[spot, :])[0:48, :].astype(BF)
+        def some(group, carry):
+            indices = [group * 8 + member for member in range(8)]
+            spots = [pl.ds(pl.multiple_of(i * 80, 8), 80) for i in indices]
+            turned = [jnp.transpose(turn_a[spot, :])[0:48, :].astype(BF) for spot in spots]
+            for i, block in zip(indices, turned, strict=True):
+                left_rot[i, :, 0:80] = block
             return carry
 
-        lax.fori_loop(0, 32, one, 0)
+        lax.fori_loop(0, 4, some, 0)
 
     def weights():
         omega = jnp.where(x_lo == 0, phonon_ref[0:1, 0:1], phonon_ref[0:1, 1:2])
         bose = 1.0 / (jnp.exp(omega / thermal) - 1.0)
         scale = (math.pi / 32.0) * (broadening / math.pi) / (2.0 * omega)
 
-        def one(i, carry):
-            there = energy_col[pl.ds(pl.multiple_of(i * 40, 8), 40), :]
-            here = energy_row[pl.ds(i, 1), :]
-            filling = 1.0 / (1.0 + jnp.exp(there / thermal))
-            spacing = here - there
-            plus = spacing + omega
-            minus = spacing - omega
-            wide = broadening * broadening
-            weight[pl.ds(pl.multiple_of(i * 40, 8), 40), :] = scale * (
-                (bose + filling) / (plus * plus + wide)
-                + (bose + 1.0 - filling) / (minus * minus + wide)
-            )
+        wide = broadening * broadening
+
+        def some(group, carry):
+            spots = [pl.ds(pl.multiple_of((group * 8 + i) * 40, 8), 40) for i in range(8)]
+            rows = energy_row[pl.ds(pl.multiple_of(group * 8, 8), 8), :]
+            gains = scale * length_row[pl.ds(pl.multiple_of(group * 8, 8), 8), :]
+            found = []
+            for i, spot in enumerate(spots):
+                there = energy_col[spot, :]
+                filling = 1.0 / (1.0 + jnp.exp(there / thermal))
+                spacing = rows[i : i + 1, :] - there
+                plus = spacing + omega
+                minus = spacing - omega
+                found.append(
+                    gains[i : i + 1, :]
+                    * (
+                        (bose + filling) / (plus * plus + wide)
+                        + (bose + 1.0 - filling) / (minus * minus + wide)
+                    )
+                )
+            for spot, value in zip(spots, found, strict=True):
+                weight[spot, :] = value
             return carry
 
-        lax.fori_loop(0, 32, one, 0)
+        lax.fori_loop(0, 4, some, 0)
 
     def electron_phases():
         lane4 = iota((128, 128), 1)
@@ -549,7 +583,7 @@
         )
 
     def some_points(group, carry):
-        indices = [group * 8 + i for i in range(8)]
+        indices = [group * 16 + i for i in range(16)]
         spots = [pl.ds(pl.multiple_of(i * 40, 8), 40) for i in indices]
         turned = [
             mm(coupling[spot, 0:80].astype(BF), right_rot[i])
@@ -565,23 +599,24 @@
             jnp.sum(f * f * weight[spot, 0:80], axis=0, keepdims=True)
             for f, spot in zip(final, spots, strict=True)
         ]
-        rates[pl.ds(pl.multiple_of(group * 8, 8), 8), 0:80] = jnp.concatenate(sums, axis=0)
+        rates[pl.ds(pl.multiple_of(group * 16, 8), 16), 0:80] = jnp.concatenate(sums, axis=0)
         return carry
 
-    lax.fori_loop(0, 4, some_points, 0)
-
-    for b in (0, 1):
-        rows = rates[b * 16 : b * 16 + 16, 0:40] + rates[b * 16 : b * 16 + 16, 40:80]
+    rates[...] = jnp.zeros((32, 128), F32)
+    c_copies = []
+    for dl in (0, 1):
+        b = (x_lo + dl) % 2
+        some_points(b, 0)
+        rows = rates[pl.ds(pl.multiple_of(b * 16, 16), 16), :]
+        rows = rows[:, 0:40] + rows[:, 40:80]
         rates_b[b] = jnp.concatenate([rows[0:8], rows[8:16], jnp.zeros((8, 48), F32)], axis=1)
-    c_copies = []
-    for dx in (1, 0):
-        for dl in (1, 0):
+        for dx in (1, 0):
             for dc in (1, 0):
                 spot = dx * 4 + dc * 2 + dl
                 if spot == 0:
                     continue
                 copy = remote(
-                    rates_b.at[(x_lo + dl) % 2],
+                    rates_b.at[b],
                     land_c.at[spot],
                     rc_s.at[spot],
                     rc_r.at[spot],
@@ -674,6 +709,7 @@
             vm((32, 48, 128), BF),
             vm((1280, 128), F32),
             vm((32, 128), F32),
+            vm((32, 128), F32),
             vm((1280, 128), F32),
             vm((1280, 128), F32),
             vm((32, 128), F32),
@@ -681,7 +717,7 @@
             vm((8, 8, 128), F32),
             vm((8, 128), F32),
             vm((8, 8, 128), F32),
-            dma(11),
+            dma(14),
             dma(2),
             dma(2),
             pltpu.SemaphoreType.DMA,

time: 59.2 us -> 56.2 us (0.949); the launches traced: 58.3 us -> 56 us
  Pallas kernels: 57 us -> 54.7 us
    pallas_call x1, Pallas kernels: 57 us -> 54.7 us  [per_device(): pl.pallas_call(kernel, out_shape=jax.ShapeDtypeStruct((16, 40), F32), in_...]
where the time goes in v4:
time: 56.2 us; the launch traced here: 56 us
  Pallas kernels  54.7 us (97%)
  local copies, waits for them, and re-layouts  1.3 us (2%)
    pallas_call x1, Pallas kernels, per_device(): pl.pallas_call(kernel, out_shape=jax.ShapeDtypeStruct((16, 40), F32), in_...  54.7 us
    unnamed x1, local copies, waits for them, and re-layouts  1.3 us

profile of v4, /device:TPU:1, one launch (start us, length us, event | category | flops | bytes accessed | tf_op | source)
XLA Modules:
  0.0 56.0 jit_solution(16418928538828710525)
XLA Ops:
  0.0 54.7 %shard_map.109 = f32[16,40]{1,0:T(8,128)} custom-call(bf16[4,4,6400]{2,1,0:T(4,128)(2,1)} %w_hbm.1, s32[4,3]{1,0:T(4,128)} %plat_hbm.1, s32[1,4]{1,0:T(1,128)} %bitcast.8, s32[3,64]{1,0:T(4,128)} %bitcast.5, s32[1,64]{1,0:T(1,128)} %bitcast.9, f32[3,32]{1,0:T(4,128)} %bitcast.6, f32[3,16]{1,0:T(4,128)} %bitcast.7, f32[1,2]{1,0:T(1,128)} %phonon_hbm.1, ...), custom_call_target="tpu_custom_call" | custom-call | flops 300000000 | bytes 2000000 | tf_op jit(solution)/shard_map/pallas_call | solution.py:667
  54.7 1.3 %copy.13 = f32[16,40]{1,0:T(8,128)} copy(f32[16,40]{1,0:T(8,128)} %shard_map.109) | data formatting | bytes 5120

commit v5 on v4

--- a/solution.py
+++ b/solution.py
@@ -71,8 +71,7 @@
     rot_ref,
     band_ref,
     shift_ref,
-    w_own,
-    w_sib,
+    w_both,
     cosw,
     sinw,
     lhs_own,
@@ -220,14 +219,18 @@
     loaded("w0", "w1", "w2", "w3")
     cells = jnp.concatenate([w_ref[e].astype(F32) for e in range(4)], axis=0)
     for mc in range(4):
-        w_own[mc * 16 : mc * 16 + 16, :] = jnp.concatenate(
+        w_both[mc * 16 : mc * 16 + 16, :] = jnp.concatenate(
             [cells[:, mc * ROW : (mc + 1) * ROW], jnp.zeros((16, LANES - ROW), F32)], axis=1
         ).astype(BF)
 
     pl.semaphore_wait(barrier, len(partners))
 
     sib = flip_rp(0, 1)
-    core_copies = [remote(w_own, w_sib, core_s.at[0], core_r.at[0], sib, re)]
+    core_copies = [
+        remote(
+            w_both.at[0:64], w_both.at[64:128], core_s.at[0], core_r.at[0], sib, re
+        )
+    ]
 
     loaded("plat", "pdeg", "qvec")
     r_of_lane = jnp.where(iota((4, 128), 0) == (iota((4, 128), 1) & 3), 1.0, 0.0).astype(F32)
@@ -239,7 +242,7 @@
     sinw[...] = (jnp.sin(p_angle) * p_weight).astype(BF)
     row = iota((256, 128), 0)
     lane = iota((256, 128), 1)
-    same = ((row >> 3) & 1 == (lane >> 5) & 1) & (row & 3 == (lane >> 2) & 3) & (lane < 64)
+    same = ((row >> 3) & 1 == (lane >> 5) & 1) & (row & 3 == (lane >> 2) & 3)
     to_imag = (row >> 2) & 1
     of_imag = (lane >> 4) & 1
     pick_cos = same & (to_imag == of_imag)
@@ -248,40 +251,42 @@
     q_row = iota((256, 32), 0)
     q_lane = iota((256, 32), 1)
 
-    def phases_for(which_core):
+    def phases_for(which_core, lanes):
         spread = jnp.where((q_row >> 4) * 2 + which_core == q_lane, 1.0, 0.0).astype(BF)
         cos_part = mm(spread, cosw[...])
         sin_part = mm(spread, sinw[...])
         return jnp.where(
-            pick_cos, cos_part, jnp.where(pick_sin, sign * sin_part, 0.0)
+            pick_cos & lanes, cos_part, jnp.where(pick_sin & lanes, sign * sin_part, 0.0)
         ).astype(BF)
 
-    lhs_out[...] = phases_for(1 - core)
+    lhs_out[...] = phases_for(1 - core, lane >= 64)
 
     core_copies.append(remote(lhs_out, lhs_sib, core_s.at[1], core_r.at[1], sib, re))
-    lhs_own[...] = phases_for(core)
-    for start, end in LANE_TILES:
-        part[:, start:end] = mm(lhs_own[:, 0:64], w_own[:, start:end])
+    lhs_own[...] = phases_for(core, lane < 64)
     for copy in core_copies:
         copy.wait_recv()
-    for start, end in LANE_TILES:
-        part[:, start:end] += mm(lhs_sib[:, 0:64], w_sib[:, start:end])
-
-    def part_of(z_to, sub):
+    lhs_own[...] += lhs_sib[...]
+
+    def lhs_of(z_to, sub):
         hi = (1 - x_hi) if sub == 0 else x_hi
         block = ((z_to + 8) % 8) * 2 + hi
-        return part[pl.ds(pl.multiple_of(block * 16, 16), 16), :]
-
+        return lhs_own[pl.ds(pl.multiple_of(block * 16, 16), 16), :]
+
+    outer_lhs = jnp.concatenate([lhs_of(z + s, sub) for s in (4, 3, -3) for sub in (0, 1)], axis=0)
+    for start, end in LANE_TILES:
+        block = mm(outer_lhs, w_both[:, start:end]).astype(BF)
+        for sub in (0, 1):
+            s_opp[sub, :, start:end] = block[sub * 16 : sub * 16 + 16]
+            s_far[0, sub, :, start:end] = block[32 + sub * 16 : 48 + sub * 16]
+            s_far[1, sub, :, start:end] = block[64 + sub * 16 : 80 + sub * 16]
     far = {}
     opp = {}
     for sub in (0, 1):
         toward = 2 if sub == 0 else -2
-        s_opp[sub] = part_of(z + 4, sub).astype(BF)
         opp[sub] = remote(
             s_opp.at[sub], l_opp.at[sub], opp_s.at[sub], opp_r.at[sub], along_z(toward), re
         )
         for side, step in ((0, 1), (1, -1)):
-            s_far[side, sub] = part_of(z + 3 * step, sub).astype(BF)
             far[side, sub] = remote(
                 s_far.at[side, sub],
                 l_far.at[side, sub],
@@ -290,11 +295,14 @@
                 along_z(step),
                 re,
             )
-
-    def piece_of(z_to, dx, dl):
-        hi = (1 - x_hi) if dx else x_hi
-        mode = (x_lo + dl) % 2
-        first_row = (((z_to + 8) % 8) * 2 + hi) * 16 + mode * 8
+    inner_lhs = jnp.concatenate(
+        [lhs_of(z + s, sub) for s in (0, 1, -1, 2, -2) for sub in (0, 1)], axis=0
+    )
+    for start, end in LANE_TILES:
+        part[:, start:end] = mm(inner_lhs, w_both[:, start:end])
+
+    def piece_of(place, dx, dl):
+        first_row = place * 32 + (1 - dx) * 16 + ((x_lo + dl) % 2) * 8
         rows = part[pl.ds(pl.multiple_of(first_row, 8), 8), :]
         end = jnp.concatenate([rows[:, HALF:], jnp.zeros((8, 2 * HALF - LANES), F32)], axis=1)
         return jnp.concatenate([rows[:, 0:HALF], end], axis=0).astype(BF)
@@ -302,7 +310,7 @@
     pieces = {}
 
     def send_piece(place, step, dx, dl):
-        s_piece[dl, dx, place] = piece_of(z + step, dx, dl)
+        s_piece[dl, dx, place] = piece_of(place, dx, dl)
         pieces[dl, dx, place] = remote(
             s_piece.at[dl, dx, place],
             l_piece.at[dl, dx, place],
@@ -386,9 +394,8 @@
             if side == sub:
                 opp[sub].wait_recv()
                 more = more + l_opp[sub].astype(F32)
-            hi = (1 - x_hi) if sub == 0 else x_hi
-            block = ((z + 8 + 2 * step) % 8) * 2 + hi
-            part[pl.ds(pl.multiple_of(block * 16, 16), 16), :] += more
+            first_row = (3 + side) * 32 + sub * 16
+            part[first_row : first_row + 16, :] += more
             for dl in (1, 0):
                 send_piece(3 + side, 2 * step, 1 - sub, dl)
 
@@ -520,7 +527,7 @@
     u_swap = remote(u_in.at[x_lo], u_in.at[x_lo], swap_s, swap_r, rp, flip_re(1))
     for copy in pieces.values():
         copy.wait_recv()
-    own_row = (z * 2 + x_hi) * 16 + x_lo * 8
+    own_row = 16 + x_lo * 8
     blocks = []
     for dl in (0, 1):
         added = None
@@ -537,40 +544,40 @@
     waves[0] = jnp.concatenate(blocks, axis=0).astype(BF)
 
     first = {}
-    for place, step in ((2, 1), (1, -1), (4, 2), (3, -2)):
+    for place, step in ((4, 2), (3, -2), (2, 1), (1, -1)):
         first[place] = remote(
             waves.at[0], waves.at[place], y1_s.at[place], y1_r.at[place], rp, along_y(step)
         )
-    first[2].wait_recv()
-    later = [remote(waves.at[2], waves.at[6], y2_s.at[0], y2_r.at[0], rp, along_y(2))]
-    first[1].wait_recv()
-    later.append(remote(waves.at[1], waves.at[5], y2_s.at[1], y2_r.at[1], rp, along_y(-2)))
     lower = pl.ds(0, HALF)
     upper = pl.ds(HALF, LANES - HALF)
-    first[4].wait_recv()
-    later.append(
-        remote(
-            waves.at[4, :, lower],
-            waves.at[7, :, lower],
-            y2_s.at[2],
-            y2_r.at[2],
-            rp,
-            along_y(2),
-        )
-    )
-    first[3].wait_recv()
-    later.append(
-        remote(
-            waves.at[3, :, upper],
-            waves.at[7, :, upper],
-            y2_s.at[3],
-            y2_r.at[3],
-            rp,
-            along_y(-2),
-        )
-    )
+    later = []
+    for number, (place, lanes, step) in enumerate(((4, lower, 1), (3, upper, -1))):
+        first[place].wait_recv()
+        later.append(
+            remote(
+                waves.at[place, :, lanes],
+                waves.at[7, :, lanes],
+                y2_s.at[number],
+                y2_r.at[number],
+                rp,
+                along_y(2 * step),
+            )
+        )
+    for number, (place, to, step) in enumerate(((4, 6, 1), (3, 5, -1))):
+        later.append(
+            remote(
+                waves.at[place],
+                waves.at[to],
+                y2_s.at[2 + number],
+                y2_r.at[2 + number],
+                rp,
+                along_y(step),
+            )
+        )
     rotations_there()
     weights()
+    first[2].wait_recv()
+    first[1].wait_recv()
     points_c = mm(mix[:, 0:80], waves[0:5].reshape(80, LANES))
     for copy in later:
         copy.wait_recv()
@@ -681,8 +688,7 @@
             vm((16, 3200), F32),
             vm((16, 40), F32),
             vm((1, 256), jnp.int32),
-            vm((64, LANES), BF),
-            vm((64, LANES), BF),
+            vm((128, LANES), BF),
             vm((32, 128), BF),
             vm((32, 128), BF),
             vm((256, 128), BF),
@@ -694,7 +700,7 @@
             vm((2, 144, PACK), BF),
             vm((8, 2, 16, PACK), BF),
             vm((2, 8, 2, 16, PACK), BF),
-            vm((256, LANES), F32),
+            vm((160, LANES), F32),
             vm((2, 2, 16, LANES), BF),
             vm((2, 2, 16, LANES), BF),
             vm((2, 16, LANES), BF),

time: 56.2 us -> 53.8 us (0.957)
  Pallas kernels: 54.7 us -> 52.3 us
    pallas_call x1, Pallas kernels: 54.7 us -> 52.3 us  [per_device(): pl.pallas_call(kernel, out_shape=jax.ShapeDtypeStruct((16, 40), F32), in_...]
where the time goes in v5:
time: 53.8 us; the launch traced here: 53.6 us
  Pallas kernels  52.3 us (97%)
  local copies, waits for them, and re-layouts  1.3 us (2%)
    pallas_call x1, Pallas kernels, per_device(): pl.pallas_call(kernel, out_shape=jax.ShapeDtypeStruct((16, 40), F32), in_...  52.3 us
    unnamed x1, local copies, waits for them, and re-layouts  1.3 us

profile of v5, /device:TPU:1, one launch (start us, length us, event | category | flops | bytes accessed | tf_op | source)
XLA Modules:
  0.0 53.6 jit_solution(2867510672847189362)
XLA Ops:
  0.0 52.3 %shard_map.109 = f32[16,40]{1,0:T(8,128)} custom-call(bf16[4,4,6400]{2,1,0:T(4,128)(2,1)} %w_hbm.1, s32[4,3]{1,0:T(4,128)} %plat_hbm.1, s32[1,4]{1,0:T(1,128)} %bitcast.8, s32[3,64]{1,0:T(4,128)} %bitcast.5, s32[1,64]{1,0:T(1,128)} %bitcast.9, f32[3,32]{1,0:T(4,128)} %bitcast.6, f32[3,16]{1,0:T(4,128)} %bitcast.7, f32[1,2]{1,0:T(1,128)} %phonon_hbm.1, ...), custom_call_target="tpu_custom_call" | custom-call | flops 300000000 | bytes 2000000 | tf_op jit(solution)/shard_map/pallas_call | solution.py:674
  52.3 1.3 %copy.13 = f32[16,40]{1,0:T(8,128)} copy(f32[16,40]{1,0:T(8,128)} %shard_map.109) | data formatting | bytes 5120

commit v6 on v5

--- a/solution.py
+++ b/solution.py
@@ -223,15 +223,6 @@
             [cells[:, mc * ROW : (mc + 1) * ROW], jnp.zeros((16, LANES - ROW), F32)], axis=1
         ).astype(BF)
 
-    pl.semaphore_wait(barrier, len(partners))
-
-    sib = flip_rp(0, 1)
-    core_copies = [
-        remote(
-            w_both.at[0:64], w_both.at[64:128], core_s.at[0], core_r.at[0], sib, re
-        )
-    ]
-
     loaded("plat", "pdeg", "qvec")
     r_of_lane = jnp.where(iota((4, 128), 0) == (iota((4, 128), 1) & 3), 1.0, 0.0).astype(F32)
     p_angle = full_turn * outer(qvec_ref[...], outer(plat_ref[...].astype(F32), r_of_lane))
@@ -260,6 +251,15 @@
         ).astype(BF)
 
     lhs_out[...] = phases_for(1 - core, lane >= 64)
+
+    pl.semaphore_wait(barrier, len(partners))
+
+    sib = flip_rp(0, 1)
+    core_copies = [
+        remote(
+            w_both.at[0:64], w_both.at[64:128], core_s.at[0], core_r.at[0], sib, re
+        )
+    ]
 
     core_copies.append(remote(lhs_out, lhs_sib, core_s.at[1], core_r.at[1], sib, re))
     lhs_own[...] = phases_for(core, lane < 64)
@@ -673,7 +673,7 @@
 
     return pl.pallas_call(
         kernel,
-        out_shape=jax.ShapeDtypeStruct((16, 40), F32),
+        out_shape=pltpu.VMEM((16, 40), F32),
         in_specs=[pl.BlockSpec(memory_space=pl.ANY)] * 11,
         out_specs=pl.BlockSpec(memory_space=pltpu.VMEM),
         scratch_shapes=[

time: 53.8 us -> 52.1 us (0.968)
  Pallas kernels: 52.3 us -> 51.4 us
  local copies, waits for them, and re-layouts: 1.3 us -> 0.6 us
    pallas_call x1, Pallas kernels: 52.3 us -> 51.4 us  [per_device(): pl.pallas_call(kernel, out_shape=pltpu.VMEM((16, 40), F32), in_specs=[pl....]
    unnamed x1, local copies, waits for them, and re-layouts: 1.3 us -> 0.6 us
where the time goes in v6:
time: 52.1 us; the launch traced here: 52 us
  Pallas kernels  51.4 us (99%)
  local copies, waits for them, and re-layouts  0.6 us (1%)
    pallas_call x1, Pallas kernels, per_device(): pl.pallas_call(kernel, out_shape=pltpu.VMEM((16, 40), F32), in_specs=[pl....  51.4 us

profile of v6, /device:TPU:1, one launch (start us, length us, event | category | flops | bytes accessed | tf_op | source)
XLA Modules:
  0.0 52.0 jit_solution(15774277268662510083)
XLA Ops:
  0.0 51.4 %shard_map.109 = f32[16,40]{1,0:T(8,128)S(1)} custom-call(bf16[4,4,6400]{2,1,0:T(4,128)(2,1)} %w_hbm.1, s32[4,3]{1,0:T(4,128)} %plat_hbm.1, s32[1,4]{1,0:T(1,128)} %bitcast.8, s32[3,64]{1,0:T(4,128)} %bitcast.5, s32[1,64]{1,0:T(1,128)} %bitcast.9, f32[3,32]{1,0:T(4,128)} %bitcast.6, f32[3,16]{1,0:T(4,128)} %bitcast.7, f32[1,2]{1,0:T(1,128)} %phonon_hbm.1, ...), custom_call_target="tpu_custom_call" | custom-call | flops 300000000 | bytes 2000000 | tf_op jit(solution)/shard_map/pallas_call | solution.py:674
  51.4 0.6 %copy.13 = f32[16,40]{1,0:T(8,128)} copy(f32[16,40]{1,0:T(8,128)S(1)} %shard_map.109) | data formatting | bytes 5120

commit v7 on v6

--- a/solution.py
+++ b/solution.py
@@ -373,7 +373,7 @@
     take = jnp.where(take, 1.0, 0.0).astype(BF)
     u_out[...] = mm(take, pack[0:128, :]).astype(BF).reshape(8, 2, 16, PACK)
     u_copies = []
-    for step in (4, 3, 5, 2, 6, 1, 7):
+    for step in (1, 7, 2, 6, 3, 5, 4):
         u_copies.append(
             remote(
                 u_out.at[(y + step) % 8],
@@ -525,21 +525,23 @@
     for copy in u_copies:
         copy.wait_recv()
     u_swap = remote(u_in.at[x_lo], u_in.at[x_lo], swap_s, swap_r, rp, flip_re(1))
-    for copy in pieces.values():
-        copy.wait_recv()
-    own_row = 16 + x_lo * 8
+    def add_pieces(dl, places, added):
+        for dx in (0, 1):
+            for place in places:
+                if (dl, dx, place) not in pieces:
+                    continue
+                pieces[dl, dx, place].wait_recv()
+                piece = l_piece[dl, dx, place].astype(F32)
+                added = piece if added is None else added + piece
+        return added
+
+    nearer = [add_pieces(dl, (0, 1, 2), None) for dl in (0, 1)]
     blocks = []
     for dl in (0, 1):
-        added = None
-        for dx in (0, 1):
-            for place in range(5):
-                if dl == 0 and dx == 0 and place == 0:
-                    continue
-                piece = l_piece[dl, dx, place].astype(F32)
-                added = piece if added is None else added + piece
+        added = add_pieces(dl, (3, 4), nearer[dl])
         block = jnp.concatenate([added[0:8], added[8:16, 0 : LANES - HALF]], axis=1)
         if dl == 0:
-            block = block + part[pl.ds(pl.multiple_of(own_row, 8), 8), :]
+            block = block + part[pl.ds(pl.multiple_of(16 + x_lo * 8, 8), 8), :]
         blocks.append(block)
     waves[0] = jnp.concatenate(blocks, axis=0).astype(BF)
 

time: 52.1 us -> 52 us (level)
  no operation moved by 1% of the time
where the time goes in v7:
time: 52 us; the launch traced here: 51.9 us
  Pallas kernels  51.3 us (99%)
  local copies, waits for them, and re-layouts  0.6 us (1%)
    pallas_call x1, Pallas kernels, per_device(): pl.pallas_call(kernel, out_shape=pltpu.VMEM((16, 40), F32), in_specs=[pl....  51.3 us

profile of v7, /device:TPU:1, one launch (start us, length us, event | category | flops | bytes accessed | tf_op | source)
XLA Modules:
  0.0 51.9 jit_solution(6041231300837293040)
XLA Ops:
  0.0 51.3 %shard_map.109 = f32[16,40]{1,0:T(8,128)S(1)} custom-call(bf16[4,4,6400]{2,1,0:T(4,128)(2,1)} %w_hbm.1, s32[4,3]{1,0:T(4,128)} %plat_hbm.1, s32[1,4]{1,0:T(1,128)} %bitcast.8, s32[3,64]{1,0:T(4,128)} %bitcast.5, s32[1,64]{1,0:T(1,128)} %bitcast.9, f32[3,32]{1,0:T(4,128)} %bitcast.6, f32[3,16]{1,0:T(4,128)} %bitcast.7, f32[1,2]{1,0:T(1,128)} %phonon_hbm.1, ...), custom_call_target="tpu_custom_call" | custom-call | flops 300000000 | bytes 2000000 | tf_op jit(solution)/shard_map/pallas_call | solution.py:676
  51.3 0.6 %copy.13 = f32[16,40]{1,0:T(8,128)} copy(f32[16,40]{1,0:T(8,128)S(1)} %shard_map.109) | data formatting | bytes 5120

commit v8 on v7

--- a/solution.py
+++ b/solution.py
@@ -225,10 +225,14 @@
 
     loaded("plat", "pdeg", "qvec")
     r_of_lane = jnp.where(iota((4, 128), 0) == (iota((4, 128), 1) & 3), 1.0, 0.0).astype(F32)
-    p_angle = full_turn * outer(qvec_ref[...], outer(plat_ref[...].astype(F32), r_of_lane))
-    p_weight = 1.0 / jnp.dot(
-        pdeg_ref[...].astype(F32), r_of_lane, precision=highest, preferred_element_type=F32
+    lattice = lax.dot_general(
+        plat_ref[...].astype(F32).astype(BF),
+        r_of_lane.astype(BF),
+        (((0,), (0,)), ((), ())),
+        preferred_element_type=F32,
     )
+    p_angle = full_turn * outer(qvec_ref[...], lattice)
+    p_weight = 1.0 / mm(pdeg_ref[...].astype(F32).astype(BF), r_of_lane.astype(BF))
     cosw[...] = (jnp.cos(p_angle) * p_weight).astype(BF)
     sinw[...] = (jnp.sin(p_angle) * p_weight).astype(BF)
     row = iota((256, 128), 0)

time: 52 us -> 52 us (level)
  no operation moved by 1% of the time
where the time goes in v8:
time: 52 us; the launch traced here: 51.9 us
  Pallas kernels  51.3 us (99%)
  local copies, waits for them, and re-layouts  0.6 us (1%)
    pallas_call x1, Pallas kernels, per_device(): pl.pallas_call(kernel, out_shape=pltpu.VMEM((16, 40), F32), in_specs=[pl....  51.3 us

profile of v8, /device:TPU:1, one launch (start us, length us, event | category | flops | bytes accessed | tf_op | source)
XLA Modules:
  0.0 51.9 jit_solution(8718819729659478268)
XLA Ops:
  0.0 51.3 %shard_map.109 = f32[16,40]{1,0:T(8,128)S(1)} custom-call(bf16[4,4,6400]{2,1,0:T(4,128)(2,1)} %w_hbm.1, s32[4,3]{1,0:T(4,128)} %plat_hbm.1, s32[1,4]{1,0:T(1,128)} %bitcast.8, s32[3,64]{1,0:T(4,128)} %bitcast.5, s32[1,64]{1,0:T(1,128)} %bitcast.9, f32[3,32]{1,0:T(4,128)} %bitcast.6, f32[3,16]{1,0:T(4,128)} %bitcast.7, f32[1,2]{1,0:T(1,128)} %phonon_hbm.1, ...), custom_call_target="tpu_custom_call" | custom-call | flops 300000000 | bytes 2000000 | tf_op jit(solution)/shard_map/pallas_call | solution.py:680
  51.3 0.6 %copy.13 = f32[16,40]{1,0:T(8,128)} copy(f32[16,40]{1,0:T(8,128)S(1)} %shard_map.109) | data formatting | bytes 5120
